TPU v7x, 32 devices: a whole 2x2x4 slice. The times are simulated.
32 devices in a mesh: seq: 8 (over z, x), dp: 4 (over y, core).
Axes of the slice: x: 2, y: 2, z: 4, core: 2. Of those that a mesh axis runs over, the one named last changes fastest.
Arguments:
- tokens: bfloat16 [4, 8192, 768], P('dp', 'seq'), may hold values from -8 to 8
- tile_mask: int32 [4, 8192], P('dp', 'seq'), may hold values from 0 to 1, as said below
- cotangent: bfloat16 [4, 8192, 768], P('dp', 'seq'), may hold values from -6 to 6
- qkv_weight: bfloat16 [768, 2304], replicated, may hold values from -0.21875 to 0.21875
- proj_weight: bfloat16 [768, 768], replicated, may hold values from -6 to 6
- proj_bias: bfloat16 [768], replicated, may hold values from -4 to 4
- up_weight: bfloat16 [768, 3072], replicated, may hold values from -0.21875 to 0.21875
- up_bias: bfloat16 [3072], replicated, may hold values from -4 to 4
- down_weight: bfloat16 [3072, 768], replicated, may hold values from -0.109375 to 0.109375
- down_bias: bfloat16 [768], replicated, may hold values from -4 to 4
- attn_gain: bfloat16 [768], replicated, may hold values from 0.5 to 1.5
- attn_shift: bfloat16 [768], replicated, may hold values from -4 to 4
- mlp_gain: bfloat16 [768], replicated, may hold values from 0.5 to 1.5
- mlp_shift: bfloat16 [768], replicated, may hold values from -4 to 4
- mask_vector: bfloat16 [768], replicated, may hold values from -5 to 5
Outputs:
- layer_out: bfloat16 [4, 8192, 768], P('dp', 'seq')
- tokens_grad: bfloat16 [4, 8192, 768], P('dp', 'seq')
- qkv_grad: float32 [768, 2304], P('seq')
- proj_grad: float32 [768, 768], P('seq')
- proj_bias_grad: float32 [768], P('seq')
- up_grad: float32 [768, 3072], P('seq')
- up_bias_grad: float32 [3072], P('seq')
- down_grad: float32 [3072, 768], P('seq')
- down_bias_grad: float32 [768], P('seq')
- attn_gain_grad: float32 [768], P('seq')
- attn_shift_grad: float32 [768], P('seq')
- mlp_gain_grad: float32 [768], P('seq')
- mlp_shift_grad: float32 [768], P('seq')
- mask_vector_grad: float32 [768], P('seq')
- stream_rms: float32 [3], replicated
Inputs may be any that keep to these rules, and one draw needn't show every extreme that they name: `tile_mask`: in each slide the share of hidden tiles is drawn between a half and three quarters.
All inputs are finite; a program needn't handle non-finite values.
Results may differ from a plain program's by a relative error of at most 0.014.
Values may be sent and summed in bfloat16 or wider, within the bound.
No kernel may reach another device: no remote copies, remote signals or barrier semaphores. Data moves between devices by JAX's collectives and lax.ppermute only.
A program may use at most 320 MiB of HBM per device.

v0:
```python
import jax
import jax.numpy as jnp
from jax import lax
from jax.sharding import PartitionSpec as P

HEADS = 16
BRANCHES = 4


EPS = 1e-06
FILL = -1e30


def for_sending(array):
    return jax.tree.map(lambda a: a.astype(jnp.bfloat16) if a.dtype == jnp.float32 else a, array)


def swapped(value, axis, distance):
    mask = 2**distance
    pairs = [(source, source ^ mask) for source in range(lax.axis_size(axis))]
    return lax.ppermute(value, axis, pairs)


def layer_norm(inputs, scales, offsets):
    average = jnp.mean(inputs, axis=-1, keepdims=True)
    centred = inputs - average
    spread = jnp.mean(centred * centred, axis=-1, keepdims=True)
    return centred * lax.rsqrt(spread + EPS) * scales + offsets


def gelu_exact(inputs):
    return jax.nn.gelu(inputs, approximate=False)


def dilate(field_in, dilation):
    row_count, middle_count, head_count, last_count = field_in.shape
    shaped = field_in.reshape(
        row_count // dilation, dilation, middle_count, head_count // dilation, dilation, last_count
    )
    diagonal = jnp.diagonal(shaped, axis1=1, axis2=4)
    return jnp.moveaxis(diagonal, -1, 0)


def undilate(unit_rows, dilation, filler):
    moved = jnp.moveaxis(unit_rows, 0, 1)
    select = jnp.eye(dilation, dtype=bool)[None, :, None, None, :, None]
    spread_out = jnp.where(select, moved[:, :, :, :, None, :], filler)
    return spread_out.reshape(
        moved.shape[0] * dilation, moved.shape[2], moved.shape[3] * dilation, moved.shape[4]
    )


def regroup(payload, dilation, mover):
    position = lax.axis_index("seq")
    for bit_index in range(dilation.bit_length() - 1):
        is_upper = position >> bit_index & 1 == 1
        outgoing = []
        staying = []
        for member in payload:
            shaped = member.reshape(
                (dilation >> bit_index + 1, 2, 1 << bit_index) + member.shape[1:]
            )
            outgoing.append(jnp.where(is_upper, shaped[:, 0], shaped[:, 1]))
            staying.append(jnp.where(is_upper, shaped[:, 1], shaped[:, 0]))
        arrived = mover(tuple(outgoing), bit_index)
        payload = tuple(
            (
                jnp.stack(
                    [
                        jnp.where(is_upper, received_half, kept_half),
                        jnp.where(is_upper, kept_half, received_half),
                    ],
                    axis=1,
                ).reshape(member.shape)
                for received_half, kept_half, member in zip(arrived, staying, payload)
            )
        )
    return payload


def move_queries(payload, bit_index):
    return jax.tree.map(
        lambda part, own: part.astype(own.dtype),
        swapped(for_sending(payload), "seq", bit_index),
        payload,
    )


def move_outputs(payload, bit_index):
    return jax.tree.map(
        lambda part, own: part.astype(own.dtype),
        swapped(for_sending(payload), "seq", bit_index),
        payload,
    )


def move_grads(payload, bit_index):
    return jax.tree.map(
        lambda part, own: part.astype(own.dtype),
        swapped(for_sending(payload), "seq", bit_index),
        payload,
    )


def move_grads_back(payload, bit_index):
    return jax.tree.map(
        lambda part, own: part.astype(own.dtype),
        swapped(for_sending(payload), "seq", bit_index),
        payload,
    )


def attend_heads(queries, key_rows, value_rows):
    scale = queries.shape[-1] ** (-0.5)

    def one_head(triple):
        query_head, key_head, value_head = triple
        scores = jnp.dot(query_head, key_head.T, preferred_element_type=jnp.float32) * scale
        totals = jax.nn.logsumexp(scores, axis=-1)
        probs = jnp.exp(scores - totals[:, None]).astype(jnp.bfloat16)
        return (jnp.dot(probs, value_head, preferred_element_type=jnp.float32), totals)

    return lax.map(one_head, (queries, key_rows, value_rows))


def attend_back(queries, key_rows, value_rows, grad_out, grad_total):
    scale = queries.shape[-1] ** (-0.5)

    def one_head(bundle):
        query_head, key_head, value_head, grad_head, total_head = bundle
        scores = jnp.dot(query_head, key_head.T, preferred_element_type=jnp.float32) * scale
        totals = jax.nn.logsumexp(scores, axis=-1)
        probs = jnp.exp(scores - totals[:, None])
        probs_low = probs.astype(jnp.bfloat16)
        grad_probs = jnp.dot(grad_head, value_head.T, preferred_element_type=jnp.float32)
        inner = jnp.sum(probs * grad_probs, axis=-1, keepdims=True)
        grad_scores = (probs * (grad_probs - inner + total_head[:, None])).astype(jnp.bfloat16)
        grad_query = jnp.dot(grad_scores, key_head, preferred_element_type=jnp.float32) * scale
        grad_keys = jnp.dot(grad_scores.T, query_head, preferred_element_type=jnp.float32) * scale
        grad_values = jnp.dot(probs_low.T, grad_head, preferred_element_type=jnp.float32)
        return (grad_query, grad_keys, grad_values)

    return lax.map(one_head, (queries, key_rows, value_rows, grad_out, grad_total))


def gather_units(split_qkv, dilation, row_count, head_count, head_dim):
    (arrived,) = regroup((dilate(split_qkv, dilation),), dilation, move_queries)
    local_units = arrived.reshape(row_count, 3, head_count // dilation, head_dim)
    return jnp.transpose(local_units, (1, 2, 0, 3))


def local(
    tokens,
    tile_mask,
    cotangent,
    qkv_weight,
    proj_weight,
    proj_bias,
    up_weight,
    up_bias,
    down_weight,
    down_bias,
    attn_gain,
    attn_shift,
    mlp_gain,
    mlp_shift,
    mask_vector,
):
    stream = tokens[0].astype(jnp.float32)
    row_count, model_width = stream.shape
    head_count = HEADS
    head_dim = model_width // head_count
    hidden_rows = (tile_mask[0] == 1)[:, None]
    start = jnp.where(hidden_rows, mask_vector.astype(jnp.float32)[None, :], stream)
    normed, norm_back = jax.vjp(
        layer_norm, start, attn_gain.astype(jnp.float32), attn_shift.astype(jnp.float32)
    )
    normed_low = normed.astype(jnp.bfloat16)
    qkv = jnp.dot(normed_low, qkv_weight, preferred_element_type=jnp.float32).astype(jnp.bfloat16)
    split_qkv = qkv.reshape(row_count, 3, head_count, head_dim)
    kept_units = []
    branch_outs = []
    branch_totals = []
    for branch in range(BRANCHES):
        dilation = 2**branch
        heads_first = gather_units(split_qkv, dilation, row_count, head_count, head_dim)
        kept_units.append(heads_first)
        outputs, totals = attend_heads(heads_first[0], heads_first[1], heads_first[2])
        out_units = jnp.transpose(outputs.astype(jnp.bfloat16), (1, 0, 2)).reshape(
            dilation, row_count // dilation, 1, head_count // dilation, head_dim
        )
        total_units = jnp.transpose(totals, (1, 0)).reshape(
            dilation, row_count // dilation, 1, head_count // dilation, 1
        )
        out_back, total_back = regroup((out_units, total_units), dilation, move_outputs)
        branch_outs.append(undilate(out_back, dilation, 0.0)[:, 0].astype(jnp.float32))
        branch_totals.append(undilate(total_back, dilation, FILL)[:, 0, :, 0])
    stacked_totals = jnp.stack(branch_totals)
    peak = jnp.max(stacked_totals, axis=0)
    weights = jnp.exp(stacked_totals - peak)
    shares = weights / jnp.sum(weights, axis=0)
    merged = jnp.sum(shares[..., None] * jnp.stack(branch_outs), axis=0)
    attn_low = merged.reshape(row_count, model_width).astype(jnp.bfloat16)
    middle = (
        start
        + jnp.dot(attn_low, proj_weight, preferred_element_type=jnp.float32)
        + proj_bias.astype(jnp.float32)
    )
    normed2, norm2_back = jax.vjp(
        layer_norm, middle, mlp_gain.astype(jnp.float32), mlp_shift.astype(jnp.float32)
    )
    normed2_low = normed2.astype(jnp.bfloat16)
    pre = jnp.dot(normed2_low, up_weight, preferred_element_type=jnp.float32) + up_bias.astype(
        jnp.float32
    )
    act, gelu_back = jax.vjp(gelu_exact, pre)
    act_low = act.astype(jnp.bfloat16)
    final = (
        middle
        + jnp.dot(act_low, down_weight, preferred_element_type=jnp.float32)
        + down_bias.astype(jnp.float32)
    )
    layer_out = final.astype(jnp.bfloat16)[None]
    visible = 1.0 - hidden_rows.astype(jnp.float32)
    local_sums = jnp.stack(
        [
            jnp.sum(visible * stream * stream),
            jnp.sum(visible * middle * middle),
            jnp.sum(visible * final * final),
        ]
    )
    total_sums, visible_count = lax.psum((local_sums, jnp.sum(visible)), ("seq", "dp"))
    stream_rms = jnp.sqrt(total_sums / (visible_count * model_width))
    grad_final = cotangent[0].astype(jnp.float32)
    grad_mlp = grad_final.astype(jnp.bfloat16)
    down_grad = jnp.dot(act_low.T, grad_mlp, preferred_element_type=jnp.float32)
    down_bias_grad = jnp.sum(grad_mlp.astype(jnp.float32), axis=0)
    grad_act = jnp.dot(grad_mlp, down_weight.T, preferred_element_type=jnp.float32)
    (grad_pre,) = gelu_back(grad_act)
    grad_pre_low = grad_pre.astype(jnp.bfloat16)
    up_grad = jnp.dot(normed2_low.T, grad_pre_low, preferred_element_type=jnp.float32)
    up_bias_grad = jnp.sum(grad_pre_low.astype(jnp.float32), axis=0)
    grad_normed2 = jnp.dot(grad_pre_low, up_weight.T, preferred_element_type=jnp.float32)
    grad_mid_norm, mlp_gain_grad, mlp_shift_grad = norm2_back(grad_normed2)
    grad_middle = grad_final + grad_mid_norm
    grad_branch = grad_middle.astype(jnp.bfloat16)
    proj_grad = jnp.dot(attn_low.T, grad_branch, preferred_element_type=jnp.float32)
    proj_bias_grad = jnp.sum(grad_branch.astype(jnp.float32), axis=0)
    grad_merged = jnp.dot(grad_branch, proj_weight.T, preferred_element_type=jnp.float32).reshape(
        row_count, head_count, head_dim
    )
    grad_total_qkv = jnp.zeros((row_count, 3, head_count, head_dim), jnp.float32)
    for branch in range(BRANCHES):
        dilation = 2**branch
        branch_share = shares[branch]
        grad_out_b = (branch_share[..., None] * grad_merged).astype(jnp.bfloat16)
        grad_lse_b = branch_share * jnp.sum(grad_merged * (branch_outs[branch] - merged), axis=-1)
        grad_units, lse_units = regroup(
            (dilate(grad_out_b[:, None], dilation), dilate(grad_lse_b[:, None, :, None], dilation)),
            dilation,
            move_grads,
        )
        grad_heads = jnp.transpose(
            grad_units.reshape(row_count, head_count // dilation, head_dim), (1, 0, 2)
        )
        lse_heads = jnp.transpose(lse_units.reshape(row_count, head_count // dilation), (1, 0))
        heads_first = kept_units[branch]
        grad_query, grad_keys, grad_values = attend_back(
            heads_first[0], heads_first[1], heads_first[2], grad_heads, lse_heads
        )
        stacked = jnp.stack([grad_query, grad_keys, grad_values], axis=1)
        stacked = jnp.transpose(stacked, (2, 1, 0, 3)).reshape(
            dilation, row_count // dilation, 3, head_count // dilation, head_dim
        )
        (returned,) = regroup((stacked,), dilation, move_grads_back)
        grad_total_qkv = grad_total_qkv + undilate(returned, dilation, 0.0)
    grad_qkv_low = grad_total_qkv.reshape(row_count, 3 * model_width).astype(jnp.bfloat16)
    qkv_grad = jnp.dot(normed_low.T, grad_qkv_low, preferred_element_type=jnp.float32)
    grad_normed = jnp.dot(grad_qkv_low, qkv_weight.T, preferred_element_type=jnp.float32)
    grad_start_norm, attn_gain_grad, attn_shift_grad = norm_back(grad_normed)
    grad_start = grad_middle + grad_start_norm
    tokens_grad = jnp.where(hidden_rows, 0.0, grad_start).astype(jnp.bfloat16)[None]
    mask_vector_grad = jnp.sum(jnp.where(hidden_rows, grad_start, 0.0), axis=0)
    pieces = (
        qkv_grad,
        proj_grad,
        proj_bias_grad,
        up_grad,
        up_bias_grad,
        down_grad,
        down_bias_grad,
        attn_gain_grad,
        attn_shift_grad,
        mlp_gain_grad,
        mlp_shift_grad,
        mask_vector_grad,
    )
    seq_count = lax.axis_size("seq")
    blocks = jnp.concatenate([piece.reshape(seq_count, -1) for piece in pieces], axis=1)
    share_part = lax.psum_scatter(blocks, "seq", scatter_dimension=0, tiled=True)
    share_part = lax.psum(share_part.astype(jnp.bfloat16), "dp").astype(jnp.float32)
    summed = share_part.reshape(-1)
    results = []
    offset = 0
    for piece in pieces:
        length = piece.size // seq_count
        results.append(
            summed[offset : offset + length].reshape(
                (piece.shape[0] // seq_count,) + piece.shape[1:]
            )
        )
        offset = offset + length
    return (
        layer_out,
        tokens_grad,
        results[0],
        results[1],
        results[2],
        results[3],
        results[4],
        results[5],
        results[6],
        results[7],
        results[8],
        results[9],
        results[10],
        results[11],
        stream_rms,
    )


def solution(mesh):
    in_specs = (
        P("dp", "seq", None),
        P("dp", "seq"),
        P("dp", "seq", None),
        P(),
        P(),
        P(),
        P(),
        P(),
        P(),
        P(),
        P(),
        P(),
        P(),
        P(),
        P(),
    )
    out_specs = (
        P("dp", "seq", None),
        P("dp", "seq", None),
        P("seq", None),
        P("seq", None),
        P("seq"),
        P("seq", None),
        P("seq"),
        P("seq", None),
        P("seq"),
        P("seq"),
        P("seq"),
        P("seq"),
        P("seq"),
        P("seq"),
        P(),
    )
    return jax.shard_map(local, mesh=mesh, in_specs=in_specs, out_specs=out_specs, check_vma=False)
```

profile of v0, /device:TPU:0, one launch (start us, length us, event | category | flops | bytes accessed | tf_op | source)
XLA Modules:
  0.0 3099.5 jit_solution(11416124578108785704)
XLA Ops:
  24.6 19.9 reshape_reshape.114
  44.5 16.3 copy.1681
  69.3 19.9 reshape_reshape.109
  89.2 18.9 copy.1662
  114.2 19.9 reshape_reshape.106
  134.1 29.2 copy.1651
  176.8 6.6 copy.1647
  202.2 102.1 %while.112 = (s32[]{:T(128)}, bf16[16,1024,48]{1,2,0:T(8,128)(2,1)}, f32[16,1024]{1,0:T(8,128)}, bf16[16,1024,48]{2,1,0:T(8,128)(2,1)}, bf16[16,1024,48]{2,1,0:T(8,128)(2,1)}, /*index=5*/bf16[16,1024,48]{2,1,0:T(8,128)(2,1)}) while((s32[]{:T(128)}, bf16[16,1024,48]{1,2,0:T(8,128)(2,1)}, f32[16,1024]{1,0:T(8,128)}, ...), condition=%wide.region_5.6_spmd.clone, body=%wide.region_2.5_spmd.sunk.clone | while | flops 209722368 | bytes 13629521 | solution.py:123
  357.2 12.8 while.115
  418.9 29.0 while.114
  463.0 6.8 reshape_reshape.107
  481.0 55.5 %while.113 = (s32[]{:T(128)}, bf16[8,1024,48]{1,2,0:T(8,128)(2,1)}, f32[8,1024]{1,0:T(8,128)}, bf16[8,1024,48]{2,1,0:T(8,128)(2,1)}, bf16[8,1024,48]{2,1,0:T(8,128)(2,1)}, /*index=5*/bf16[8,1024,48]{2,1,0:T(8,128)(2,1)}) while((s32[]{:T(128)}, bf16[8,1024,48]{1,2,0:T(8,128)(2,1)}, f32[8,1024]{1,0:T(8,128)}, ...), condition=%wide.region_9.10_spmd.clone, body=%wide.region_6.9_spmd.sunk.clone | while | flops 209722368 | bytes 13629521 | solution.py:123
  710.1 35.8 %multiply_convert_fusion.4 = (bf16[1024,3072]{1,0:T(8,128)(2,1)}, f32[1024,3072]{1,0:T(8,128)}, f32[1024,3072]{1,0:T(8,128)}) fusion(f32[3072]{0:T(1024)S(1)} %copy-done.119, bf16[768,3072]{1,0:T(8,128)(2,1)S(1)} %bitcast.1635, f32[1024,768]{0,1:T(8,128)S(1)} %get-tuple-element.1267, f32[768]{0:T(1024)S(1)} %copy-done.123, f32[768]{0:T(1024)S(1)} %copy-done.110, ...), kind=kOutput, calls=%fused_computation.259 | convolution fusion | flops 5043388416 | bytes 39348224 | tf_op jit(solution)/shard_map/dot_general | solution.py:213
  745.9 19.2 convert_reduce_fusion
  765.1 10.5 fusion.377
  775.6 7.8 fusion.359
  787.2 14.7 fusion.240
  811.2 7.9 fusion.252
  822.7 7.8 reshape.2536
  830.4 10.4 reshape.2532
  840.8 15.9 reshape.2528
  867.4 7.1 multiply_reduce_fusion.15
  902.0 6.2 reshape.2658
  916.6 7.8 copy.1805
  935.4 8.4 copy.1774
  953.5 12.0 copy.1749
  965.4 6.6 copy.1740
  972.0 7.4 fusion.213
  979.4 216.2 %while.116 = (s32[]{:T(128)}, f32[16,1024,48]{1,2,0:T(8,128)}, f32[16,1024,48]{1,2,0:T(8,128)}, f32[16,1024,48]{1,2,0:T(8,128)}, bf16[16,1024,48]{2,1,0:T(8,128)...) while((s32[]{:T(128)}, f32[16,1024,48]{1,2,0:T(8,128)}, ...), condition=%wide.region_29.30_spmd.clone, body=%wide.region_25.29_spmd.sunk.clone | while | flops 522292224 | bytes 38147176 | solution.py:143
  1233.5 16.7 while.119
  1264.3 50.7 %while.118 = (s32[]{:T(128)}, f32[4,1024,48]{1,2,0:T(8,128)}, f32[4,1024,48]{1,2,0:T(8,128)}, f32[4,1024,48]{1,2,0:T(8,128)}, bf16[4,1024,48]{2,1,0:T(8,128)(2,1...) while((s32[]{:T(128)}, f32[4,1024,48]{1,2,0:T(8,128)}, ...), condition=%wide.region_41.42_spmd.clone, body=%wide.region_37.41_spmd.sunk.clone | while | flops 522292224 | bytes 39392388 | solution.py:143
  1336.9 107.1 %while.117 = (s32[]{:T(128)}, f32[8,1024,48]{1,2,0:T(8,128)}, f32[8,1024,48]{1,2,0:T(8,128)}, f32[8,1024,48]{1,2,0:T(8,128)}, bf16[8,1024,48]{2,1,0:T(8,128)(2,1...) while((s32[]{:T(128)}, f32[8,1024,48]{1,2,0:T(8,128)}, ...), condition=%wide.region_35.36_spmd.clone, body=%wide.region_31.35_spmd.sunk.clone | while | flops 522292224 | bytes 37819496 | solution.py:143
  1449.1 7.5 reshape_reshape.126
  1456.7 8.7 fusion.366
  1470.0 7.1 collective-permute-done.34
  1491.0 9.0 reshape.2543
  1504.8 8.9 reshape.2545
  1521.9 10.4 broadcast_in_dim.604
  1532.3 20.6 broadcast_in_dim.605
  1552.9 17.7 copy.1844
  1570.5 9.6 copy.1840
  1584.0 6.8 copy.1800
  1597.3 10.9 copy.1769
  1608.3 17.0 broadcast_in_dim.591
  1625.3 40.3 %broadcast_in_dim.592 = f32[1024,2304]{1,0:T(8,128)} reshape(f32[512,2,3,8,2,48]{5,4,3,2,1,0:T(2,128)} %broadcast_in_dim.591) | data formatting | bytes 18874368 | tf_op jit(solution)/shard_map/jit(_where)/broadcast_in_dim | solution.py:47
  1665.6 17.7 copy.1842
  1683.3 9.6 copy.1770
  1692.9 15.3 broadcast_in_dim.598
  1708.3 29.4 broadcast_in_dim.599
  1737.6 17.7 copy.1843
  1755.3 9.7 copy.1801
  1765.1 14.1 fusion.212
  1779.3 6.4 fusion.249
  1785.7 7.2 reshape.2540
  1792.9 14.4 fusion.209
  1839.7 26.5 dynamic-update-slice.3
  1867.6 26.1 dynamic-update-slice.5
  1902.2 1064.3 %all-reduce.6 = bf16[8,885792]{1,0:T(8,128)(2,1)} all-reduce(f32[8,885792]{1,0:T(8,128)} %dynamic-update-slice.11), channel_id=2, replica_groups=mesh['seq'=8,'dp'=4] {'seq'}, use_global_device_ids=true, to_apply=%region_58.59.clone | all-reduce | flops 7086336 | bytes 42518016
  2966.5 8.8 dynamic-slice_convert_fusion
  2981.2 40.4 %all-reduce.1 = (f32[3]{0:T(128)S(1)}, f32[]{:T(128)}) all-reduce(f32[3]{0:T(128)S(1)} %pad_maximum_fusion.27, f32[]{:T(128)} %fusion.350), channel_id=1, replica_groups=mesh['seq'=8,'dp'=4] {'seq','dp'}, use_global_device_ids=true, to_apply=%region_63.64 | all-reduce | flops 4 | bytes 32 | tf_op jit(solution)/shard_map/psum | solution.py:232
  3025.3 25.3 all-reduce.5.cloned.1.call-done
  3050.6 6.3 convert_element_type.650
  3059.6 10.1 slice_reduce_fusion.2
  3069.7 13.9 slice_reduce_fusion
  (1243 shorter events, 1219.1 us)
Async XLA Ops:
  7.2 11.5 copy-start
  7.2 3043.4 %all-reduce.5.cloned.1.call-start = ((), (), s32[]{:S(2)}) async-start(), calls=%async_computation | async-start | bytes 7087104 | tf_op jit(solution)/shard_map/psum | solution.py:301
  7.3 53.5 %copy-start.75 = (s32[8]{0:T(128)}, s32[8]{0:T(128)S(1)}, u32[]{:S(2)}) copy-start(s32[8]{0:T(128)S(1)} %or_bitcast_fusion) | copy-start | bytes 100
  66.3 238.6 %collective-permute-start.6 = (bf16[4,1,128,3,2,48]{2,5,4,3,0,1:T(8,128)(2,1)}, bf16[4,1,128,3,2,48]{2,5,4,3,0,1:T(8,128)(2,1)}, u32[]{:S(2)}, u32[]{:S(2)}) collective-permute-start(bf16[4,1,128,3,2,48]{2,5,4,3,0,1:T(8,128)(2,1)} %fusion.293), channel_id=1, source_target_pairs={{0,4},{4,0},{8,12},{12,8},{16,20},{20,16},{24,28},{28,24},{1,5},{5... | collective-permute-start | bytes 884744 | tf_op jit(solution)/shard_map/ppermute | solution.py:21
  69.3 38.8 %copy-start.86 = (s32[4]{0:T(128)}, s32[4]{0:T(128)S(1)}, u32[]{:S(2)}) copy-start(s32[4]{0:T(128)S(1)} %or_bitcast_fusion.1) | copy-start | bytes 52
  114.2 228.2 %collective-permute-start.2 = (bf16[2,1,256,3,4,48]{2,5,4,3,0,1:T(8,128)(2,1)}, bf16[2,1,256,3,4,48]{2,5,4,3,0,1:T(8,128)(2,1)}, u32[]{:S(2)}, u32[]{:S(2)}) collective-permute-start(bf16[2,1,256,3,4,48]{2,5,4,3,0,1:T(8,128)(2,1)} %fusion.282), channel_id=1, source_target_pairs={{0,4},{4,0},{8,12},{12,8},{16,20},{20,16},{24,28},{28,24},{1,5},{5... | collective-permute-start | bytes 1769480 | tf_op jit(solution)/shard_map/ppermute | solution.py:21
  114.2 49.0 %copy-start.106 = (s32[2]{0:T(128)}, s32[2]{0:T(128)S(1)}, u32[]{:S(2)}) copy-start(s32[2]{0:T(128)S(1)} %or_bitcast_fusion.2) | copy-start | bytes 28
  170.9 285.9 %collective-permute-start = (bf16[1,1,512,3,8,48]{2,5,3,4,1,0:T(8,128)(2,1)}, bf16[1,1,512,3,8,48]{2,5,3,4,1,0:T(8,128)(2,1)}, u32[]{:S(2)}, u32[]{:S(2)}) collective-permute-start(bf16[1,1,512,3,8,48]{2,5,3,4,1,0:T(8,128)(2,1)} %get-tuple-element.1170), channel_id=1, source_target_pairs={{0,4},{4,0},{8,12},{12,8},{16,20},{20,16},{24,28},{28,24},{1,5},{5... | collective-permute-start | bytes 3538952 | tf_op jit(solution)/shard_map/ppermute | solution.py:21
  172.9 151.9 %copy-start.127 = (pred[8,8]{0,1:T(8,128)(4,1)}, pred[8,8]{0,1:T(8,128)(4,1)S(1)}, u32[]{:S(2)}) copy-start(pred[8,8]{0,1:T(8,128)(4,1)S(1)} %iota_compare_fusion) | copy-start | bytes 196
  202.2 102.1 %copy-start.91 = (pred[1024]{0:T(1024)(128)(4,1)S(1)}, pred[1024]{0:T(1024)(128)(4,1)}, u32[]{:S(2)}) copy-start(pred[1024]{0:T(1024)(128)(4,1)} %copy-done.90) | copy-start | bytes 3076
  304.3 28.7 copy-start.128
  306.2 8.0 collective-permute-start.7
  310.0 14.3 copy-start.120
  316.0 29.1 collective-permute-start.8
  338.5 358.6 %copy-start.64 = (pred[1024,16]{0,1:T(8,128)(4,1)}, pred[1024,16]{0,1:T(8,128)(4,1)S(1)}, u32[]{:S(2)}) copy-start(pred[1024,16]{0,1:T(8,128)(4,1)S(1)} %broadcast_in_dim.562) | copy-start | bytes 49156
  372.1 3.7 collective-permute-start.9
  377.0 4.6 collective-permute-start.10
  379.4 29.1 collective-permute-start.3
  382.4 7.0 collective-permute-start.11
  385.6 5.9 collective-permute-start.15
  393.8 11.0 collective-permute-start.16
  407.5 140.4 %collective-permute-start.17 = (bf16[1,4,128,1,2,48]{2,5,4,1,3,0:T(8,128)(2,1)}, bf16[1,4,128,1,2,48]{2,5,4,1,3,0:T(8,128)(2,1)}, u32[]{:S(2)}, u32[]{:S(2)}) collective-permute-start(bf16[1,4,128,1,2,48]{2,5,4,1,3,0:T(8,128)(2,1)} %fusion.315), channel_id=1, source_target_pairs={{0,16},{4,20},{8,24},{12,28},{16,0},{20,4},{24,8},{28,12},{1,17},{... | collective-permute-start | bytes 294920 | tf_op jit(solution)/shard_map/ppermute | solution.py:21
  451.2 97.6 %collective-permute-start.4 = (bf16[2,1,256,1,4,1]{2,4,0,5,3,1:T(4,128)(2,1)}, bf16[2,1,256,1,4,1]{2,4,0,5,3,1:T(4,128)(2,1)}, u32[]{:S(2)}, u32[]{:S(2)}) collective-permute-start(bf16[2,1,256,1,4,1]{2,4,0,5,3,1:T(4,128)(2,1)} %fusion.346), channel_id=1, source_target_pairs={{0,4},{4,0},{8,12},{12,8},{16,20},{20,16},{24,28},{28,24},{1,5},{5... | collective-permute-start | bytes 12296 | tf_op jit(solution)/shard_map/ppermute | solution.py:21
  455.6 164.6 %collective-permute-start.13 = (bf16[2,1,256,1,4,48]{2,5,4,3,1,0:T(8,128)(2,1)}, bf16[2,1,256,1,4,48]{2,5,4,3,1,0:T(8,128)(2,1)}, u32[]{:S(2)}, u32[]{:S(2)}) collective-permute-start(bf16[2,1,256,1,4,48]{2,5,4,3,1,0:T(8,128)(2,1)} %bitcast.1275), channel_id=1, source_target_pairs={{0,4},{4,0},{8,12},{12,8},{16,20},{20,16},{24,28},{28,24},{1,5},{5... | collective-permute-start | bytes 589832 | tf_op jit(solution)/shard_map/ppermute | solution.py:21
  541.1 45.1 %collective-permute-start.1 = (bf16[1,1,512,1,8,1]{2,4,5,3,1,0:T(8,128)(2,1)}, bf16[1,1,512,1,8,1]{2,4,5,3,1,0:T(8,128)(2,1)}, u32[]{:S(2)}, u32[]{:S(2)}) collective-permute-start(bf16[1,1,512,1,8,1]{2,4,5,3,1,0:T(8,128)(2,1)} %fusion.331), channel_id=1, source_target_pairs={{0,4},{4,0},{8,12},{12,8},{16,20},{20,16},{24,28},{28,24},{1,5},{5... | collective-permute-start | bytes 24584 | tf_op jit(solution)/shard_map/ppermute | solution.py:21
  546.6 132.2 %collective-permute-start.12 = (bf16[1,1,512,1,8,48]{2,5,4,3,1,0:T(8,128)(2,1)}, bf16[1,1,512,1,8,48]{2,5,4,3,1,0:T(8,128)(2,1)}, u32[]{:S(2)}, u32[]{:S(2)}) collective-permute-start(bf16[1,1,512,1,8,48]{2,5,4,3,1,0:T(8,128)(2,1)} %select_bitcast_fusion.8), channel_id=1, source_target_pairs={{0,4},{4,0},{8,12},{12,8},{16,20},{20,16},{24,28},{28,24},{1,5},{5... | collective-permute-start | bytes 1179656 | tf_op jit(solution)/shard_map/ppermute | solution.py:21
  550.2 20.1 collective-permute-start.5
  624.1 38.3 %collective-permute-start.14 = (bf16[1,2,256,1,4,48]{2,5,4,3,1,0:T(8,128)(2,1)}, bf16[1,2,256,1,4,48]{2,5,4,3,1,0:T(8,128)(2,1)}, u32[]{:S(2)}, u32[]{:S(2)}) collective-permute-start(bf16[1,2,256,1,4,48]{2,5,4,3,1,0:T(8,128)(2,1)} %select_bitcast_fusion.12), channel_id=1, source_target_pairs={{0,8},{4,12},{8,0},{12,4},{16,24},{20,28},{24,16},{28,20},{1,9},{5... | collective-permute-start | bytes 589832 | tf_op jit(solution)/shard_map/ppermute | solution.py:21
  709.3 66.3 %copy-start.25 = (f32[1024,768]{0,1:T(8,128)}, f32[1024,768]{0,1:T(8,128)S(1)}, u32[]{:S(2)}) copy-start(f32[1024,768]{0,1:T(8,128)S(1)} %get-tuple-element.1267) | copy-start | bytes 9437188
  710.1 65.5 %copy-start.111 = (f32[1024]{0:T(1024)}, f32[1024]{0:T(1024)S(1)}, u32[]{:S(2)}) copy-start(f32[1024]{0:T(1024)S(1)} %fusion.352) | copy-start | bytes 12292
  787.1 14.8 copy-start.26
  787.2 14.8 copy-start.27
  787.2 14.8 copy-start.112
  874.5 11.8 copy-start.76
  889.0 313.2 %collective-permute-start.30 = (bf16[4,1,128,1,2,1]{2,0,4,5,3,1:T(4,128)(2,1)}, bf16[4,1,128,1,2,1]{2,0,4,5,3,1:T(4,128)(2,1)}, u32[]{:S(2)}, u32[]{:S(2)}) collective-permute-start(bf16[4,1,128,1,2,1]{2,0,4,5,3,1:T(4,128)(2,1)} %fusion.356), channel_id=1, source_target_pairs={{0,4},{4,0},{8,12},{12,8},{16,20},{20,16},{24,28},{28,24},{1,5},{5... | collective-permute-start | bytes 6152 | tf_op jit(solution)/shard_map/ppermute | solution.py:21
  900.0 309.0 %collective-permute-start.23 = (bf16[2,1,256,1,4,1]{2,4,0,5,3,1:T(4,128)(2,1)}, bf16[2,1,256,1,4,1]{2,4,0,5,3,1:T(4,128)(2,1)}, u32[]{:S(2)}, u32[]{:S(2)}) collective-permute-start(bf16[2,1,256,1,4,1]{2,4,0,5,3,1:T(4,128)(2,1)} %fusion.344), channel_id=1, source_target_pairs={{0,4},{4,0},{8,12},{12,8},{16,20},{20,16},{24,28},{28,24},{1,5},{5... | collective-permute-start | bytes 12296 | tf_op jit(solution)/shard_map/ppermute | solution.py:21
  916.6 302.1 %collective-permute-start.19 = (bf16[1,1,512,1,8,1]{2,4,5,3,1,0:T(8,128)(2,1)}, bf16[1,1,512,1,8,1]{2,4,5,3,1,0:T(8,128)(2,1)}, u32[]{:S(2)}, u32[]{:S(2)}) collective-permute-start(bf16[1,1,512,1,8,1]{2,4,5,3,1,0:T(8,128)(2,1)} %fusion.332), channel_id=1, source_target_pairs={{0,4},{4,0},{8,12},{12,8},{16,20},{20,16},{24,28},{28,24},{1,5},{5... | collective-permute-start | bytes 24584 | tf_op jit(solution)/shard_map/ppermute | solution.py:21
  933.4 286.1 %collective-permute-start.27 = (bf16[4,1,128,1,2,48]{2,5,4,3,1,0:T(8,128)(2,1)}, bf16[4,1,128,1,2,48]{2,5,4,3,1,0:T(8,128)(2,1)}, u32[]{:S(2)}, u32[]{:S(2)}) collective-permute-start(bf16[4,1,128,1,2,48]{2,5,4,3,1,0:T(8,128)(2,1)} %bitcast.1276), channel_id=1, source_target_pairs={{0,4},{4,0},{8,12},{12,8},{16,20},{20,16},{24,28},{28,24},{1,5},{5... | collective-permute-start | bytes 294920 | tf_op jit(solution)/shard_map/ppermute | solution.py:21
  953.5 273.5 %collective-permute-start.21 = (bf16[2,1,256,1,4,48]{2,5,4,0,3,1:T(8,128)(2,1)}, bf16[2,1,256,1,4,48]{2,5,4,0,3,1:T(8,128)(2,1)}, u32[]{:S(2)}, u32[]{:S(2)}) collective-permute-start(bf16[2,1,256,1,4,48]{2,5,4,0,3,1:T(8,128)(2,1)} %bitcast.1274), channel_id=1, source_target_pairs={{0,4},{4,0},{8,12},{12,8},{16,20},{20,16},{24,28},{28,24},{1,5},{5... | collective-permute-start | bytes 589832 | tf_op jit(solution)/shard_map/ppermute | solution.py:21
  1202.9 4.0 collective-permute-start.31
  1206.9 123.9 %collective-permute-start.18 = (bf16[1,1,512,1,8,48]{2,5,4,3,1,0:T(8,128)(2,1)}, bf16[1,1,512,1,8,48]{2,5,4,3,1,0:T(8,128)(2,1)}, u32[]{:S(2)}, u32[]{:S(2)}) collective-permute-start(bf16[1,1,512,1,8,48]{2,5,4,3,1,0:T(8,128)(2,1)} %select_bitcast_fusion.7), channel_id=1, source_target_pairs={{0,4},{4,0},{8,12},{12,8},{16,20},{20,16},{24,28},{28,24},{1,5},{5... | collective-permute-start | bytes 1179656 | tf_op jit(solution)/shard_map/ppermute | solution.py:21
  1209.0 4.5 collective-permute-start.32
  1213.5 3.9 collective-permute-start.24
  1220.5 13.0 copy-start.85
  1220.6 4.7 collective-permute-start.28
  1225.3 5.6 collective-permute-start.29
  1229.4 30.7 collective-permute-start.22
  1260.1 205.3 %collective-permute-start.33 = (bf16[4,1,128,3,2,48]{2,5,4,3,0,1:T(8,128)(2,1)}, bf16[4,1,128,3,2,48]{2,5,4,3,0,1:T(8,128)(2,1)}, u32[]{:S(2)}, u32[]{:S(2)}) collective-permute-start(bf16[4,1,128,3,2,48]{2,5,4,3,0,1:T(8,128)(2,1)} %fusion.289), channel_id=1, source_target_pairs={{0,4},{4,0},{8,12},{12,8},{16,20},{20,16},{24,28},{28,24},{1,5},{5... | collective-permute-start | bytes 884744 | tf_op jit(solution)/shard_map/ppermute | solution.py:21
  1328.7 150.9 %collective-permute-start.25 = (bf16[2,1,256,3,4,48]{2,5,4,3,0,1:T(8,128)(2,1)}, bf16[2,1,256,3,4,48]{2,5,4,3,0,1:T(8,128)(2,1)}, u32[]{:S(2)}, u32[]{:S(2)}) collective-permute-start(bf16[2,1,256,3,4,48]{2,5,4,3,0,1:T(8,128)(2,1)} %fusion.278), channel_id=1, source_target_pairs={{0,4},{4,0},{8,12},{12,8},{16,20},{20,16},{24,28},{28,24},{1,5},{5... | collective-permute-start | bytes 1769480 | tf_op jit(solution)/shard_map/ppermute | solution.py:21
  1466.9 10.1 collective-permute-start.34
  1470.0 120.8 %collective-permute-start.20 = (bf16[1,1,512,3,8,48]{2,5,3,4,1,0:T(8,128)(2,1)}, bf16[1,1,512,3,8,48]{2,5,3,4,1,0:T(8,128)(2,1)}, u32[]{:S(2)}, u32[]{:S(2)}) collective-permute-start(bf16[1,1,512,3,8,48]{2,5,3,4,1,0:T(8,128)(2,1)} %fusion.271), channel_id=1, source_target_pairs={{0,4},{4,0},{8,12},{12,8},{16,20},{20,16},{24,28},{28,24},{1,5},{5... | collective-permute-start | bytes 3538952 | tf_op jit(solution)/shard_map/ppermute | solution.py:21
  1478.2 35.5 %collective-permute-start.35 = (bf16[1,4,128,3,2,48]{2,5,4,3,1,0:T(8,128)(2,1)}, bf16[1,4,128,3,2,48]{2,5,4,3,1,0:T(8,128)(2,1)}, u32[]{:S(2)}, u32[]{:S(2)}) collective-permute-start(bf16[1,4,128,3,2,48]{2,5,4,3,1,0:T(8,128)(2,1)} %fusion.291), channel_id=1, source_target_pairs={{0,16},{4,20},{8,24},{12,28},{16,0},{20,4},{24,8},{28,12},{1,17},{... | collective-permute-start | bytes 884744 | tf_op jit(solution)/shard_map/ppermute | solution.py:21
  1483.8 96.3 %collective-permute-start.26 = (bf16[1,2,256,3,4,48]{2,5,4,3,1,0:T(8,128)(2,1)}, bf16[1,2,256,3,4,48]{2,5,4,3,1,0:T(8,128)(2,1)}, u32[]{:S(2)}, u32[]{:S(2)}) collective-permute-start(bf16[1,2,256,3,4,48]{2,5,4,3,1,0:T(8,128)(2,1)} %fusion.279), channel_id=1, source_target_pairs={{0,8},{4,12},{8,0},{12,4},{16,24},{20,28},{24,16},{28,20},{1,9},{5... | collective-permute-start | bytes 1769480 | tf_op jit(solution)/shard_map/ppermute | solution.py:21
  1765.0 14.2 copy-start.4
  1765.0 14.2 copy-start.79
  1765.0 14.2 copy-start.83
  1765.0 14.2 copy-start.88
  1765.1 14.2 copy-start.93
  1765.1 14.2 copy-start.104
  1765.1 14.2 copy-start.122
  1839.7 26.5 copy-start.95
  1867.6 29.0 copy-start.117
  1867.6 30.4 copy-start.115
  1867.6 31.7 %copy-start.114 = (f32[8,96]{1,0:T(8,128)S(1)}, f32[8,96]{1,0:T(8,128)}, u32[]{:S(2)}) copy-start(f32[8,96]{1,0:T(8,128)} %reshape.2550) | copy-start | bytes 9220
  (131 other events, 401.4 us)
Sparse Core Ops, SparseCore 0:
  2975.4 75.1 all-reduce.4
where the time goes:
time: 3130 us; the launch traced here: 3100 us
  blocking collectives  1100 us (35%)
  local copies, waits for them, and re-layouts  1020 us (33%)
  matrix products  547 us (17%)
  other arithmetic  316 us (10%)
  waiting for transfers between devices  47.2 us (2%)
  starting transfers between devices  43.1 us (1%)
    unnamed x1, blocking collectives  1060 us
    broadcast_in_dim x39, local copies, waits for them, and re-layouts, undilate(): spread_out = jnp.where(select, moved[:, :, :, :, None, :], filler)  310 us
    another operation x6, local copies, waits for them, and re-layouts, dilate(): field_in.reshape(row_count // dilation, dilation, middle_count, head_coun...  124 us
    dot_general x60, matrix products, one_head(): jnp.dot(query_head, key_head.T, preferred_element_type=jnp.float32) * scale  105 us
    unnamed x258, local copies, waits for them, and re-layouts  101 us
    reshape x7, local copies, waits for them, and re-layouts, local(): jnp.dot(grad_branch, proj_weight.T, preferred_element_type=jnp.float32)  68.8 us
    dot_general x30, matrix products, one_head(): jnp.dot(grad_scores.T, query_head, preferred_element_type=jnp.float32)  68.3 us
    dot_general x30, matrix products, one_head(): jnp.dot(probs, value_head, preferred_element_type=jnp.float32)  67.7 us
  transfers between devices with their start and end apart: 37, of which 9 were waited for; matrix products, arithmetic and copies ran while one was open for 40% of the time, Pallas kernels for 0%

commit v1 on v0

v1 whole, which is shorter than its diff:
```python
import numpy as np
import jax
import jax.numpy as jnp
from jax import lax
from jax.experimental import pallas as pl
from jax.experimental.pallas import tpu as pltpu
from jax.sharding import PartitionSpec as P

HEADS = 16
HD = 48
AUG = 64
TILES = 1024
EPS = 1e-06
FILL = -1e30
LN2 = float(np.log(2.0))
SCALE = HD**-0.5
QSCALE = SCALE / LN2
BF = jnp.bfloat16
F32 = jnp.float32


def nn(a, b):
    return lax.dot_general(a, b, (((1,), (0,)), ((), ())), preferred_element_type=F32)


def nt(a, b):
    return lax.dot_general(a, b, (((1,), (1,)), ((), ())), preferred_element_type=F32)


def tn(a, b):
    return lax.dot_general(a, b, (((0,), (0,)), ((), ())), preferred_element_type=F32)


GROUP = 8
GROUPS = HEADS // GROUP
D = HEADS * HD
ROWS = GROUP * HD
HALF, QUARTER, EIGHTH = TILES // 2, TILES // 4, TILES // 8
MIB = 1024 * 1024


def place_of(tile):
    return (tile & 1) * HALF + (tile >> 1 & 1) * QUARTER + (tile >> 2 & 1) * EIGHTH + (tile >> 3)


def order_matrix():
    tile = np.arange(TILES)
    matrix = np.zeros((TILES, TILES), np.float32)
    matrix[tile, place_of(tile)] = 1.0
    return jnp.asarray(matrix.astype(jnp.bfloat16))


def lanes2(h):
    return (h & 1) * HALF


def lanes4(h):
    return lanes2(h) + (h >> 1 & 1) * QUARTER


def rest2(h):
    return lanes2(h) + (1 - (h >> 1 & 1)) * QUARTER


def lanes8(h):
    return lanes4(h) + (h >> 2 & 1) * EIGHTH


def weight_tables(level, compact=False):
    count = TILES >> level
    classes = 8 >> level
    totals = {0: [2.0, 3.0, 4.0], 1: [2.0, 3.0], 2: [2.0]}[level]
    lane = np.arange(count)
    key_rows = np.zeros((classes, 16, count), np.float32)
    query_rows = np.zeros((classes, 16, count), np.float32)
    key_rows[:, 3:6] = 1.0
    for c in range(classes):
        inside = np.ones(count, bool)
        before = 1.0
        for i, total in enumerate(totals):
            bit = (lane >> (9 - level - i)) & 1
            wanted = 0 if compact and i == 0 else c >> i & 1
            inside = inside & (bit == wanted)
            step = np.log2(total) - np.log2(before)
            before = total
            high = np.float32(np.asarray(step, np.float32).astype(jnp.bfloat16))
            key_rows[c, 6 + 2 * i] = inside
            key_rows[c, 7 + 2 * i] = inside
            query_rows[c, 6 + 2 * i] = inside * high
            query_rows[c, 7 + 2 * i] = inside * (step - high)
    shape = (classes * 16, count)
    return (
        jnp.asarray(key_rows.reshape(shape).astype(jnp.bfloat16)),
        jnp.asarray(query_rows.reshape(shape).astype(jnp.bfloat16)),
    )


def value_rows(count):
    row = lax.broadcasted_iota(jnp.int32, (16, count), 0)
    return jnp.where(row < 3, 1.0, 0.0).astype(BF)


def stack(*parts):
    return jnp.concatenate(parts, axis=0)


def beside(*parts):
    return jnp.concatenate(parts, axis=1)


def head_rows(j, height=HD):
    return slice(j * height, (j + 1) * height)


def attend(keys, values, queries):
    scores = nn(keys, queries)
    peak = jnp.max(scores, axis=0, keepdims=True)
    probs = jnp.exp2(scores - peak).astype(BF)
    out = nn(values, probs)
    total = out[HD : HD + 1]
    return out[:HD] / total, peak + jnp.log2(total)


def split3(value):
    high = value.astype(BF).astype(F32)
    rest = value - high
    mid = rest.astype(BF).astype(F32)
    return high, mid, rest - mid


def split_rows(*values):
    row = lax.broadcasted_iota(jnp.int32, (16, values[0].shape[1]), 0)
    packed = jnp.zeros((16, values[0].shape[1]), F32)
    for i, value in enumerate(values):
        for k, piece in enumerate(split3(value)):
            packed = jnp.where(row == 3 * i + k, piece, packed)
    return packed


def column(row, width):
    turned = jnp.broadcast_to(row, (128, row.shape[1])).T
    return jnp.concatenate([turned] * (width // 128), axis=1)


def normalise(value):
    average = jnp.mean(value, axis=1, keepdims=True)
    centred = value - average
    spread = jnp.mean(centred * centred, axis=1, keepdims=True)
    scale = lax.rsqrt(spread + EPS)
    return centred * scale, scale


def embed_kernel(
    tok_ref, mask_ref, vec_ref, w_ref, order_ref,
    normed_ref, start_ref, square_ref, qkv_ref, q4_ref, q8_ref, kv4_ref, kvr_ref,
):
    step = pl.program_id(0)

    @pl.when(step == 0)
    def _():
        hidden = column(mask_ref[...].astype(F32), D) > 0.5
        rows = tok_ref[...].astype(F32)
        start = jnp.where(hidden, vec_ref[6:7], rows)
        start_ref[...] = start.astype(BF)
        squares = jnp.where(hidden, 0.0, rows * rows)
        square_ref[...] = jnp.broadcast_to(jnp.sum(squares, axis=0, keepdims=True), (8, D))
        normed = normalise(start)[0] * vec_ref[2:3] + vec_ref[3:4]
        normed_ref[...] = tn(normed.astype(BF), order_ref[...]).astype(BF)

    value = tn(w_ref[...], normed_ref[...])

    @pl.when(step < GROUPS)
    def _():
        low = (value * QSCALE).astype(BF)
        qkv_ref[...] = low
        for j in range(GROUP):
            rows = head_rows(j)
            q4_ref[rows] = low[rows, lanes4(j) : lanes4(j) + QUARTER]
            q8_ref[rows] = low[rows, lanes8(j) : lanes8(j) + EIGHTH]

    @pl.when(step >= GROUPS)
    def _():
        low = value.astype(BF)
        qkv_ref[...] = low
        for j in range(GROUP):
            rows = head_rows(j)
            kv4_ref[rows] = low[rows, lanes4(j) : lanes4(j) + QUARTER]
            kvr_ref[rows] = low[rows, rest2(j) : rest2(j) + QUARTER]


def params(limit=24, semantics=None):
    return pltpu.CompilerParams(vmem_limit_bytes=limit * MIB)


def cost(macs, bytes_accessed, exps=0):
    return pl.CostEstimate(
        flops=int(2 * macs), bytes_accessed=int(bytes_accessed), transcendentals=int(exps)
    )


def shaped(rows, width, kind):
    return jax.ShapeDtypeStruct((rows, width), kind)


def whole(height, width):
    return pl.BlockSpec((height, width), lambda i: (0, 0))


def embed(tokens, mask_row, vectors, weight, order):
    query = lambda i: (jnp.minimum(i, GROUPS - 1), 0)
    other = lambda i: (jnp.maximum(i - GROUPS, 0), 0)
    return pl.pallas_call(
        embed_kernel,
        grid=(3 * GROUPS,),
        in_specs=[
            whole(TILES, D), whole(1, TILES), whole(16, D),
            pl.BlockSpec((D, ROWS), lambda i: (0, i)), whole(TILES, TILES),
        ],
        out_specs=[
            whole(D, TILES), whole(TILES, D), whole(8, D),
            pl.BlockSpec((ROWS, TILES), lambda i: (i, 0)),
            pl.BlockSpec((ROWS, QUARTER), query), pl.BlockSpec((ROWS, EIGHTH), query),
            pl.BlockSpec((ROWS, QUARTER), other), pl.BlockSpec((ROWS, QUARTER), other),
        ],
        out_shape=[
            shaped(D, TILES, BF), shaped(TILES, D, BF), shaped(8, D, F32),
            shaped(3 * D, TILES, BF), shaped(D, QUARTER, BF), shaped(D, EIGHTH, BF),
            shaped(2 * D, QUARTER, BF), shaped(2 * D, QUARTER, BF),
        ],
        name="embed",
        compiler_params=params(48),
        cost_estimate=cost(TILES * D * (3 * D + TILES), 20 * MIB),
    )(tokens, mask_row, vectors, weight, order)


def forward0_kernel(q_ref, k_ref, v_ref, kt_ref, qt_ref, o_ref, l_ref):
    keys = stack(k_ref[...], kt_ref[...]).T
    values = stack(v_ref[...], value_rows(TILES))
    block = 512
    for i in range(TILES // block):
        cut = slice(i * block, (i + 1) * block)
        out, total = attend(keys, values, stack(q_ref[:, cut], qt_ref[:, cut]))
        o_ref[:, cut] = out
        l_ref[0, :, cut] = total


def forward1_kernel(qa_ref, qb_ref, k4_ref, v4_ref, kr_ref, vr_ref, kt_ref, qt_ref, o_ref, l_ref):
    for j, q_ref in enumerate((qa_ref, qb_ref)):
        rows = head_rows(j)
        keys = stack(beside(k4_ref[rows], kr_ref[rows]), kt_ref[...]).T
        values = stack(beside(v4_ref[rows], vr_ref[rows]), value_rows(HALF))
        out, total = attend(keys, values, stack(q_ref[...], qt_ref[...]))
        o_ref[rows] = out
        l_ref[j] = total


def forward23_kernel(
    q2_ref, q3a_ref, q3b_ref, k4_ref, v4_ref, k4f_ref, v4f_ref, k8_ref, v8_ref, k8f_ref, v8f_ref,
    kt_ref, qt_ref, z2_ref, z3a_ref, z3b_ref,
):
    table = kt_ref[...]
    zeros = jnp.zeros((16, QUARTER), BF)
    for j in range(4):
        rows, outs = head_rows(j), head_rows(j, AUG)
        keys = beside(stack(k4_ref[rows], table), stack(k4f_ref[rows], table)).T
        values = stack(beside(v4_ref[rows], v4f_ref[rows]), value_rows(HALF))
        out, total = attend(keys, values, stack(q2_ref[rows], qt_ref[...]))
        z2_ref[outs] = stack(out, split_rows(total)).astype(BF)
        keys = stack(beside(k8_ref[rows], k8f_ref[rows]), zeros).T
        values = stack(beside(v8_ref[rows], v8f_ref[rows]), value_rows(QUARTER))
        queries = stack(beside(q3a_ref[rows], q3b_ref[rows]), zeros)
        out, total = attend(keys, values, queries)
        packed = stack(out, split_rows(total)).astype(BF)
        z3a_ref[outs] = packed[:, :EIGHTH]
        z3b_ref[outs] = packed[:, EIGHTH:]


def merge_kernel(
    o0_ref, l0_ref, o1_ref, l1_ref, z2_ref, z3a_ref, z3b_ref, a_ref, r_ref, l_ref
):
    for j in range(GROUP):
        rows, packs = head_rows(j), head_rows(j, AUG)
        start2, start4, start8 = lanes2(j), lanes4(j), lanes8(j)
        other8 = start4 + EIGHTH - (start8 - start4)

        def own(first, count):
            cut = slice(first, first + count)
            return o0_ref[rows, cut], l0_ref[j, :, cut]

        def pair(first, count):
            cut = slice(first - start2, first - start2 + count)
            return o1_ref[rows, cut], l1_ref[j, :, cut]

        def sent(ref, first, count):
            packed = ref[packs, first : first + count].astype(F32)
            return packed[:HD], jnp.sum(packed[HD : HD + 3], axis=0, keepdims=True)

        def write(first, count, parts):
            peak = parts[0][1]
            for _, total in parts[1:]:
                peak = jnp.maximum(peak, total)
            weights = [jnp.exp2(total - peak) for _, total in parts]
            weight_sum = sum(weights[1:], weights[0])
            inverse = 1.0 / weight_sum
            merged = parts[0][0] * (weights[0] * inverse)
            for (out, _), weight in zip(parts[1:], weights[1:]):
                merged = merged + out * (weight * inverse)
            cut = slice(first, first + count)
            low = merged.astype(BF)
            a_ref[rows, cut] = low
            r_ref[rows, cut] = (merged - low.astype(F32)).astype(BF)
            l_ref[j, :, cut] = peak + jnp.log2(weight_sum)

        far = HALF - start2
        cut = slice(far, far + HALF)
        low = o0_ref[rows, cut].astype(BF)
        a_ref[rows, cut] = low
        r_ref[rows, cut] = (o0_ref[rows, cut] - low.astype(F32)).astype(BF)
        l_ref[j, :, cut] = l0_ref[j, :, cut]
        first = rest2(j)
        write(first, QUARTER, [own(first, QUARTER), pair(first, QUARTER)])
        first = other8
        write(first, EIGHTH, [own(first, EIGHTH), pair(first, EIGHTH), sent(z2_ref, first - start4, EIGHTH)])
        first = start8
        write(
            first, EIGHTH,
            [own(first, EIGHTH), pair(first, EIGHTH), sent(z2_ref, first - start4, EIGHTH),
             sent(z3a_ref, 0, EIGHTH), sent(z3b_ref, 0, EIGHTH)],
        )


def rows_of(height, width, lane_block=None, first=0):
    chosen = lane_block or (lambda i: 0)
    return pl.BlockSpec((height, width), lambda i: (i + first, chosen(i)))


def table_spec(width, index):
    return pl.BlockSpec((16, width), lambda i: (index(i), 0))


def totals_spec(heads, width, first=0):
    return pl.BlockSpec((heads, 1, width), lambda i: (i + first, 0, 0))


def totals_shape(heads, width):
    return jax.ShapeDtypeStruct((heads, 1, width), F32)


PAIRS = HEADS * TILES * TILES


def forward_own(qkv, tables, group):
    first = group * GROUP
    return pl.pallas_call(
        forward0_kernel,
        grid=(GROUP,),
        in_specs=[
            rows_of(HD, TILES, None, first), rows_of(HD, TILES, None, HEADS + first),
            rows_of(HD, TILES, None, 2 * HEADS + first),
            table_spec(TILES, lambda i: i & 7), table_spec(TILES, lambda i: i & 7),
        ],
        out_specs=[rows_of(HD, TILES), totals_spec(1, TILES)],
        out_shape=[shaped(ROWS, TILES, F32), totals_shape(GROUP, TILES)],
        name="forward_own",
        compiler_params=params(),
        cost_estimate=cost(PAIRS // 2 * 600, 4 * MIB, PAIRS // 2),
    )(qkv, qkv, qkv, *tables)


def forward_pair(qkv, kv4, kvr, key_table, query_table):
    pair = rows_of(2 * HD, QUARTER)
    pair_v = rows_of(2 * HD, QUARTER, None, HEADS // 2)
    return pl.pallas_call(
        forward1_kernel,
        grid=(HEADS // 2,),
        in_specs=[
            pl.BlockSpec((HD, HALF), lambda i: (2 * i, 0)),
            pl.BlockSpec((HD, HALF), lambda i: (2 * i + 1, 1)),
            pair, pair_v, pair, pair_v,
            table_spec(HALF, lambda i: i & 3), table_spec(HALF, lambda i: i & 3),
        ],
        out_specs=[rows_of(2 * HD, HALF), totals_spec(2, HALF)],
        out_shape=[shaped(D, HALF, F32), totals_shape(HEADS, HALF)],
        name="forward_pair",
        compiler_params=params(),
        cost_estimate=cost(PAIRS // 4 * 600, 5 * MIB, PAIRS // 4),
    )(qkv, qkv, kv4, kv4, kvr, kvr, key_table, query_table)


FOUR = HEADS // 4
NEAR = (
    rows_of(4 * HD, QUARTER), rows_of(4 * HD, QUARTER, None, FOUR),
    rows_of(4 * HD, QUARTER), rows_of(4 * HD, QUARTER, None, FOUR),
    rows_of(4 * HD, EIGHTH, lambda i: i & 1), rows_of(4 * HD, EIGHTH, lambda i: i & 1, FOUR),
    rows_of(4 * HD, EIGHTH, lambda i: i & 1), rows_of(4 * HD, EIGHTH, lambda i: i & 1, FOUR),
)


def near_args(own, far):
    return (own, own, far, far, own, own, far, far)


def forward_sent(q2, q3a, q3b, own, far, tables):
    return pl.pallas_call(
        forward23_kernel,
        grid=(FOUR,),
        in_specs=[
            rows_of(4 * HD, QUARTER), rows_of(4 * HD, EIGHTH), rows_of(4 * HD, EIGHTH), *NEAR,
            table_spec(QUARTER, lambda i: i & 1), table_spec(QUARTER, lambda i: i & 1),
        ],
        out_specs=[rows_of(4 * AUG, QUARTER), rows_of(4 * AUG, EIGHTH), rows_of(4 * AUG, EIGHTH)],
        out_shape=[
            shaped(HEADS * AUG, QUARTER, BF), shaped(HEADS * AUG, EIGHTH, BF),
            shaped(HEADS * AUG, EIGHTH, BF),
        ],
        name="forward_sent",
        compiler_params=params(),
        cost_estimate=cost(PAIRS * 3 // 16 * 600, 4 * MIB, PAIRS * 3 // 16),
    )(q2, q3a, q3b, *near_args(own, far), *tables)


def merge(o0, l0, o1, l1, z2, z3a, z3b, group):
    return pl.pallas_call(
        merge_kernel,
        grid=(1,),
        in_specs=[
            whole(ROWS, TILES), totals_spec(GROUP, TILES),
            rows_of(ROWS, HALF, None, group), totals_spec(GROUP, HALF, group),
            rows_of(GROUP * AUG, QUARTER, None, group), rows_of(GROUP * AUG, EIGHTH, None, group),
            rows_of(GROUP * AUG, EIGHTH, None, group),
        ],
        out_specs=[whole(ROWS, TILES), whole(ROWS, TILES), totals_spec(GROUP, TILES)],
        out_shape=[shaped(ROWS, TILES, BF), shaped(ROWS, TILES, BF), totals_shape(GROUP, TILES)],
        name="merge",
        compiler_params=params(32),
        cost_estimate=cost(TILES * D * 10, 8 * MIB),
    )(o0, l0, o1, l1, z2, z3a, z3b)


ERFCX = (
    0.25388073921203613, 0.254069447517395, 0.22542551159858704, 0.19709868729114532,
    0.02506333962082863, 0.2244575172662735, -0.2487541288137436, 0.06875886023044586,
)


def gelu_pair(x):
    z = jnp.abs(x) * (0.5**0.5)
    t = 1.0 / (1.0 + 0.45 * z)
    series = jnp.full_like(t, 0.5 * ERFCX[-1])
    for factor in reversed(ERFCX[:-1]):
        series = series * t + 0.5 * factor
    bell = jnp.exp(-z * z)
    tail = bell * (t * series)
    below = jnp.where(x < 0.0, tail, 1.0 - tail)
    return x * below, below + x * (bell * 0.3989422804014327)


CHUNK = 768


def feed_kernel(
    order_ref, attn_a_ref, attn_b_ref, start_ref, mask_ref, cot_ref, vec_ref, proj_ref, up_ref, down_ref,
    out_ref, act_ref, pre_ref, normed_ref, attn_ref, mid_ref, sum_ref,
):
    step = pl.program_id(0)
    order = order_ref[...]
    attn = beside(nt(order, attn_a_ref[...]).astype(BF), nt(order, attn_b_ref[...]).astype(BF))
    attn_ref[...] = attn
    visible = column(1.0 - mask_ref[...].astype(F32), D)
    middle = start_ref[...].astype(F32) + nn(attn, proj_ref[...]) + vec_ref[0:1]
    hat, scale = normalise(middle)
    gain = vec_ref[4:5]
    normed = (hat * gain + vec_ref[5:6]).astype(BF)
    normed_ref[...] = normed
    cot = cot_ref[...]
    final = middle + vec_ref[1:2]
    back = jnp.zeros_like(middle)
    sums = []
    for c in range(up_ref.shape[1] // CHUNK):
        cut = slice(c * CHUNK, (c + 1) * CHUNK)
        pre = nn(normed, up_ref[:, cut]) + vec_ref[8 + c : 9 + c]
        act, slope = gelu_pair(pre)
        act = act.astype(BF)
        act_ref[:, cut] = act
        grad = (slope * nt(cot, down_ref[cut, :])).astype(BF)
        pre_ref[:, cut] = grad
        sums.append(jnp.sum(grad.astype(F32), axis=0, keepdims=True))
        final = final + nn(act, down_ref[cut, :])
        back = back + nt(grad, up_ref[:, cut])
    out_ref[...] = final.astype(BF)
    cot = cot.astype(F32)
    hat_grad = back * gain
    first = jnp.mean(hat_grad, axis=1, keepdims=True)
    second = jnp.mean(hat_grad * hat, axis=1, keepdims=True)
    mid_grad = cot + scale * (hat_grad - first - hat * second)
    mid_ref[...] = mid_grad
    for value in (
        mid_grad.astype(BF).astype(F32), cot, back * hat, back,
        visible * middle * middle, visible * final * final,
    ):
        sums.append(jnp.sum(value, axis=0, keepdims=True))
    sums.append(jnp.zeros((16 - len(sums), D), F32))
    sums = stack(*sums)

    @pl.when(step == 0)
    def _():
        sum_ref[...] = sums

    @pl.when(step > 0)
    def _():
        sum_ref[...] += sums


def once(height, width):
    return pl.BlockSpec((height, width), lambda i: (0, 0), pipeline_mode=pl.Buffered(1))


def feed(order, attn_a, attn_b, start, mask_row, cot, vectors, proj, up, down):
    ff = up.shape[1]
    block = 256
    part = lambda width: pl.BlockSpec((block, width), lambda i: (i, 0))
    return pl.pallas_call(
        feed_kernel,
        grid=(TILES // block,),
        in_specs=[
            part(TILES), once(ROWS, TILES), once(ROWS, TILES), part(D),
            pl.BlockSpec((1, block), lambda i: (0, i)), part(D), once(16, D), once(D, D),
            once(D, ff), once(ff, D),
        ],
        out_specs=[part(D), part(ff), part(ff), part(D), part(D), part(D), whole(16, D)],
        out_shape=[
            shaped(TILES, D, BF), shaped(TILES, ff, BF), shaped(TILES, ff, BF), shaped(TILES, D, BF),
            shaped(TILES, D, BF), shaped(TILES, D, F32), shaped(16, D, F32),
        ],
        name="feed",
        compiler_params=params(56),
        cost_estimate=cost(TILES * D * (4 * ff + D + TILES), 36 * MIB, TILES * ff),
    )(order, attn_a, attn_b, start, mask_row, cot, vectors, proj, up, down)


def branch_kernel(
    mid_ref, proj_ref, order_ref, a_ref, r_ref, l_ref, g_ref, g4_ref, g8_ref
):
    grad = nt(proj_ref[...], mid_ref[...].astype(BF)).astype(BF)
    grad = nn(grad, order_ref[...])
    for j in range(GROUP):
        rows, packs = head_rows(j), head_rows(j, AUG)
        merged = a_ref[rows].astype(F32) + r_ref[rows].astype(F32)
        inner = jnp.sum(grad[rows] * merged, axis=0, keepdims=True)
        packed = stack(grad[rows], split_rows(-inner, -l_ref[j])).astype(BF)
        g_ref[packs] = packed
        g4_ref[packs] = packed[:, lanes4(j) : lanes4(j) + QUARTER]
        g8_ref[packs] = packed[:, lanes8(j) : lanes8(j) + EIGHTH]


def branch(mid, proj, order, attn, rest, total, group):
    return pl.pallas_call(
        branch_kernel,
        grid=(1,),
        in_specs=[
            whole(TILES, D), rows_of(ROWS, D, None, group), whole(TILES, TILES),
            whole(ROWS, TILES), whole(ROWS, TILES), totals_spec(GROUP, TILES),
        ],
        out_specs=[whole(GROUP * AUG, TILES), whole(GROUP * AUG, QUARTER), whole(GROUP * AUG, EIGHTH)],
        out_shape=[
            shaped(GROUP * AUG, TILES, BF), shaped(GROUP * AUG, QUARTER, BF),
            shaped(GROUP * AUG, EIGHTH, BF),
        ],
        name="branch",
        compiler_params=params(40),
        cost_estimate=cost(TILES * ROWS * (D + TILES), 9 * MIB),
    )(mid, proj, order, attn, rest, total)


def weights_kernel(
    act_ref, cot_ref, normed_ref, pre_ref, attn_ref, mid_ref, out_ref, turned_n, turned_a, low, spare
):
    @pl.when(pl.program_id(0) == 0)
    def _():
        turned_n[...] = normed_ref[...].T
        turned_a[...] = attn_ref[...].T
        low[...] = mid_ref[...].astype(BF)

    block = out_ref.shape[0]
    rows = pl.ds(pl.multiple_of(pl.program_id(0) * block, block), block)
    ff = pre_ref.shape[1]
    out_ref[:, :ff] = nn(turned_n[rows], pre_ref[...]).astype(BF)
    out_ref[:, ff : ff + D] = nn(turned_a[rows], low[...]).astype(BF)
    folds = ff // D
    down = tn(act_ref[...], cot_ref[...])
    for k in range(D // 128):
        spare[k] = down[:, k * 128 : (k + 1) * 128]
    for j in range(folds):
        for k in range(D // 128):
            first = ff + D + j * D + k * 128
            piece = spare[k, pl.ds(j, block, stride=folds), :]
            out_ref[:, first : first + 128] = piece.astype(BF)


def weight_grads(act, cot, normed, pre, attn, mid):
    ff = act.shape[1]
    block = 128
    width = 2 * ff + D
    return pl.pallas_call(
        weights_kernel,
        grid=(D // block,),
        in_specs=[
            pl.BlockSpec((TILES, block * (ff // D)), lambda i: (0, i)), once(TILES, D), once(TILES, D),
            once(TILES, ff), once(TILES, D), once(TILES, D),
        ],
        out_specs=pl.BlockSpec((block, width), lambda i: (i, 0)),
        out_shape=shaped(D, width, BF),
        scratch_shapes=[
            pltpu.VMEM((D, TILES), BF), pltpu.VMEM((D, TILES), BF), pltpu.VMEM((TILES, D), BF),
            pltpu.VMEM((D // 128, block * (ff // D), 128), F32),
        ],
        name="weight_grads",
        compiler_params=params(48),
        cost_estimate=cost(TILES * D * (2 * ff + D), 32 * MIB),
    )(act, cot, normed, pre, attn, mid)


def back_block(keys, values, keys_t, queries, queries_plain, grads):
    probs = jnp.exp2(nn(keys, queries))
    grad_scores = (probs * nn(values, grads)).astype(BF)
    probs = probs.astype(BF)
    grad_q = nn(keys_t, grad_scores) * SCALE
    grad_k = nt(queries_plain, grad_scores) * LN2
    grad_v = nt(grads[:HD], probs)
    return grad_q, grad_k, grad_v


def back1_kernel(
    qa_ref, qb_ref, ga_ref, gb_ref, k4_ref, v4_ref, kr_ref, vr_ref, kt_ref, qt_ref,
    dq_ref, dk_ref, dv_ref,
):
    for j, (q_ref, g_ref) in enumerate(((qa_ref, ga_ref), (qb_ref, gb_ref))):
        rows = head_rows(j)
        keys_t = beside(k4_ref[rows], kr_ref[rows])
        keys = stack(keys_t, kt_ref[...]).T
        values = stack(beside(v4_ref[rows], vr_ref[rows]), value_rows(HALF)).T
        grads = g_ref[...]
        queries = stack(q_ref[...], grads[HD:] + qt_ref[...])
        dq_ref[rows], dk_ref[rows], dv_ref[rows] = back_block(
            keys, values, keys_t, queries, q_ref[...], grads
        )


def back23_kernel(
    q2_ref, q3a_ref, q3b_ref, g2_ref, g3a_ref, g3b_ref,
    k4_ref, v4_ref, k4f_ref, v4f_ref, k8_ref, v8_ref, k8f_ref, v8f_ref, kt_ref, qt_ref,
    dk1_ref, dv1_ref,
    dq2_ref, dq3a_ref, dq3b_ref, dk_ref, dv_ref, fara_ref, farb_ref,
):
    step = pl.program_id(0)
    table = kt_ref[...]
    row = lax.broadcasted_iota(jnp.int32, (16, QUARTER), 0)
    plain = jnp.where((row >= 3) & (row < 6), 1.0, 0.0).astype(BF)
    lane = lax.broadcasted_iota(jnp.int32, (1, QUARTER), 1)
    inside = (lane >= EIGHTH) == ((step & 1) == 1)
    for j in range(4):
        rows, packs = head_rows(j), head_rows(j, AUG)
        keys_t = beside(k4_ref[rows], k4f_ref[rows])
        keys = stack(keys_t, beside(table, table)).T
        values = stack(beside(v4_ref[rows], v4f_ref[rows]), value_rows(HALF)).T
        grads = g2_ref[packs]
        queries = stack(q2_ref[rows], grads[HD:] + qt_ref[...])
        dq, dk4, dv4 = back_block(keys, values, keys_t, queries, q2_ref[rows], grads)
        dq2_ref[rows] = dq.astype(BF)
        keys_t = beside(k8_ref[rows], k8f_ref[rows])
        keys = stack(keys_t, plain).T
        values = stack(beside(v8_ref[rows], v8f_ref[rows]), value_rows(QUARTER)).T
        grads = beside(g3a_ref[packs], g3b_ref[packs])
        plain_q = beside(q3a_ref[rows], q3b_ref[rows])
        queries = stack(plain_q, grads[HD:])
        dq, dk8, dv8 = back_block(keys, values, keys_t, queries, plain_q, grads)
        dq3a_ref[rows] = dq[:, :EIGHTH].astype(BF)
        dq3b_ref[rows] = dq[:, EIGHTH:].astype(BF)
        for kind, own_ref, one_ref, four, eight in (
            (0, dk_ref, dk1_ref, dk4, dk8),
            (1, dv_ref, dv1_ref, dv4, dv8),
        ):
            near, away = eight[:, :EIGHTH], eight[:, EIGHTH:]
            own_ref[rows] = four[:, :QUARTER] + jnp.where(inside, beside(near, near), 0.0)
            extra = four[:, QUARTER:] + jnp.where(inside, beside(away, away), 0.0)
            far = beside(one_ref[rows, :QUARTER] + extra, one_ref[rows, QUARTER:]).astype(BF)

            @pl.when(step < FOUR // GROUPS)
            def _(kind=kind, rows=rows, far=far):
                fara_ref[kind, rows] = far

            @pl.when(step >= FOUR // GROUPS)
            def _(kind=kind, rows=rows, far=far):
                farb_ref[kind, rows] = far


def back0_kernel(q_ref, g_ref, k_ref, v_ref, kt_ref, qt_ref, dq_ref, dk_ref, dv_ref):
    keys_t = k_ref[...]
    keys = stack(keys_t, kt_ref[...]).T
    values = stack(v_ref[...], value_rows(TILES)).T
    block = 512
    dk = dv = None
    for i in range(TILES // block):
        cut = slice(i * block, (i + 1) * block)
        grads = g_ref[:, cut]
        plain_q = q_ref[:, cut]
        queries = stack(plain_q, grads[HD:] + qt_ref[:, cut])
        dq, more_k, more_v = back_block(keys, values, keys_t, queries, plain_q, grads)
        dq_ref[:, cut] = dq.astype(BF)
        dk = more_k if dk is None else dk + more_k
        dv = more_v if dv is None else dv + more_v
    dk_ref[...] = dk.astype(BF)
    dv_ref[...] = dv.astype(BF)


def back_pair(qkv, grads, kv4, kvr, key_table, query_table):
    pair = rows_of(2 * HD, QUARTER)
    pair_v = rows_of(2 * HD, QUARTER, None, HEADS // 2)
    out = rows_of(2 * HD, HALF)
    even = lambda height: pl.BlockSpec((height, HALF), lambda i: (2 * i, 0))
    odd = lambda height: pl.BlockSpec((height, HALF), lambda i: (2 * i + 1, 1))
    return pl.pallas_call(
        back1_kernel,
        grid=(HEADS // 2,),
        in_specs=[
            even(HD), odd(HD), even(AUG), odd(AUG), pair, pair_v, pair, pair_v,
            table_spec(HALF, lambda i: i & 3), table_spec(HALF, lambda i: i & 3),
        ],
        out_specs=[out] * 3,
        out_shape=[shaped(D, HALF, F32)] * 3,
        name="back_pair",
        compiler_params=params(),
        cost_estimate=cost(PAIRS // 4 * 900, 12 * MIB, PAIRS // 4),
    )(qkv, qkv, grads, grads, kv4, kv4, kvr, kvr, key_table, query_table)


def back_sent(q2, q3a, q3b, g2, g3a, g3b, own, far, tables, dk1, dv1):
    quarter, eighth, half = (rows_of(4 * HD, w) for w in (QUARTER, EIGHTH, HALF))
    steps = FOUR // GROUPS
    return pl.pallas_call(
        back23_kernel,
        grid=(FOUR,),
        in_specs=[
            quarter, eighth, eighth,
            rows_of(4 * AUG, QUARTER), rows_of(4 * AUG, EIGHTH), rows_of(4 * AUG, EIGHTH), *NEAR,
            table_spec(QUARTER, lambda i: i & 1), table_spec(QUARTER, lambda i: i & 1), half, half,
        ],
        out_specs=[
            quarter, eighth, eighth, quarter, quarter,
            pl.BlockSpec((2, 4 * HD, HALF), lambda i: (0, jnp.minimum(i, steps - 1), 0)),
            pl.BlockSpec((2, 4 * HD, HALF), lambda i: (0, jnp.maximum(i - steps, 0), 0)),
        ],
        out_shape=[
            shaped(D, QUARTER, BF), shaped(D, EIGHTH, BF), shaped(D, EIGHTH, BF),
            shaped(D, QUARTER, F32), shaped(D, QUARTER, F32),
            jax.ShapeDtypeStruct((2, ROWS, HALF), BF), jax.ShapeDtypeStruct((2, ROWS, HALF), BF),
        ],
        name="back_sent",
        compiler_params=params(32),
        cost_estimate=cost(PAIRS * 3 // 16 * 900, 12 * MIB, PAIRS * 3 // 16),
    )(q2, q3a, q3b, g2, g3a, g3b, *near_args(own, far), *tables, dk1, dv1)


def back_own(qkv, grads, tables, group):
    first = group * GROUP
    full = rows_of(HD, TILES)
    return pl.pallas_call(
        back0_kernel,
        grid=(GROUP,),
        in_specs=[
            rows_of(HD, TILES, None, first), rows_of(AUG, TILES),
            rows_of(HD, TILES, None, HEADS + first), rows_of(HD, TILES, None, 2 * HEADS + first),
            table_spec(TILES, lambda i: i & 7), table_spec(TILES, lambda i: i & 7),
        ],
        out_specs=[full, full, full],
        out_shape=[shaped(ROWS, TILES, BF)] * 3,
        name="back_own",
        compiler_params=params(),
        cost_estimate=cost(PAIRS // 2 * 900, 7 * MIB, PAIRS // 2),
    )(qkv, grads, qkv, qkv, *tables)


def collect_kernel(
    dq_ref, dk_ref, dv_ref, dq1_ref, dq2_ref, dq3a_ref, dq3b_ref, dk4_ref, dv4_ref, far_ref,
    normed_ref, w_ref, grad_ref, back_ref, value_ref,
):
    step = pl.program_id(0)

    def write(base_ref, parts):
        for j in range(GROUP):
            rows = head_rows(j)
            pieces = {first: base_ref[rows, first : first + EIGHTH].astype(F32) for first in range(0, TILES, EIGHTH)}
            for ref, first, source, count in parts(j):
                for k in range(0, count, EIGHTH):
                    pieces[first + k] = pieces[first + k] + ref[rows, source + k : source + k + EIGHTH].astype(F32)
            value_ref[rows] = beside(*(pieces[first] for first in range(0, TILES, EIGHTH))).astype(BF)

    @pl.when(step == 0)
    def _():
        write(
            dq_ref,
            lambda j: (
                (dq1_ref, lanes2(j), 0, HALF), (dq2_ref, lanes4(j), 0, QUARTER),
                (dq3a_ref, lanes8(j), 0, EIGHTH), (dq3b_ref, lanes8(j), 0, EIGHTH),
            ),
        )

    for at, base_ref, own_ref, far_ref in ((1, dk_ref, dk4_ref, far_ref.at[0]), (2, dv_ref, dv4_ref, far_ref.at[1])):

        @pl.when(step == at)
        def _(base_ref=base_ref, own_ref=own_ref, far_ref=far_ref):
            write(
                base_ref,
                lambda j: (
                    (own_ref, lanes4(j), 0, QUARTER), (far_ref, lanes4(j), 0, QUARTER),
                    (far_ref, rest2(j), QUARTER, QUARTER),
                ),
            )

    value = value_ref[...]
    grad_ref[...] = nt(normed_ref[...], value).astype(BF)
    back = nn(w_ref[...], value)

    @pl.when(step == 0)
    def _():
        back_ref[...] = back

    @pl.when(step > 0)
    def _():
        back_ref[...] += back


def collect(dq, dk, dv, dq1, dq2, dq3a, dq3b, dk4, dv4, far, normed, weight, group):
    return pl.pallas_call(
        collect_kernel,
        grid=(3,),
        in_specs=[
            whole(ROWS, TILES), whole(ROWS, TILES), whole(ROWS, TILES),
            pl.BlockSpec((ROWS, HALF), lambda i: (group, 0)),
            pl.BlockSpec((ROWS, QUARTER), lambda i: (group, 0)),
            pl.BlockSpec((ROWS, EIGHTH), lambda i: (group, 0)),
            pl.BlockSpec((ROWS, EIGHTH), lambda i: (group, 0)),
            pl.BlockSpec((ROWS, QUARTER), lambda i: (group, 0)),
            pl.BlockSpec((ROWS, QUARTER), lambda i: (group, 0)),
            pl.BlockSpec((2, ROWS, HALF), lambda i: (0, 0, 0)),
            whole(D, TILES), pl.BlockSpec((D, ROWS), lambda i: (0, 2 * i + group)),
        ],
        out_specs=[pl.BlockSpec((D, ROWS), lambda i: (0, i)), whole(D, TILES)],
        out_shape=[shaped(D, 3 * ROWS, BF), shaped(D, TILES, F32)],
        scratch_shapes=[pltpu.VMEM((ROWS, TILES), BF)],
        name="collect",
        compiler_params=params(40),
        cost_estimate=cost(3 * ROWS * TILES * D * 2, 16 * MIB),
    )(dq, dk, dv, dq1, dq2, dq3a, dq3b, dk4, dv4, far, normed, weight)


def finish_kernel(back_a_ref, back_b_ref, order_ref, start_ref, mask_ref, mid_ref, vec_ref, out_ref, sum_ref):
    step = pl.program_id(0)
    turned = (back_a_ref[...] + back_b_ref[...]).astype(BF)
    back = nt(order_ref[...], turned)
    hidden = column(mask_ref[...].astype(F32), D) > 0.5
    hat, scale = normalise(start_ref[...].astype(F32))
    hat_grad = back * vec_ref[2:3]
    first = jnp.mean(hat_grad, axis=1, keepdims=True)
    second = jnp.mean(hat_grad * hat, axis=1, keepdims=True)
    grad = mid_ref[...] + scale * (hat_grad - first - hat * second)
    out_ref[...] = jnp.where(hidden, 0.0, grad).astype(BF)
    sums = stack(
        jnp.sum(back * hat, axis=0, keepdims=True),
        jnp.sum(back, axis=0, keepdims=True),
        jnp.sum(jnp.where(hidden, grad, 0.0), axis=0, keepdims=True),
        jnp.zeros((5, D), F32),
    )

    @pl.when(step == 0)
    def _():
        sum_ref[...] = sums

    @pl.when(step > 0)
    def _():
        sum_ref[...] += sums


def finish(back_a, back_b, order, start, mask_row, mid, vectors):
    block = 256
    part = lambda width: pl.BlockSpec((block, width), lambda i: (i, 0))
    return pl.pallas_call(
        finish_kernel,
        grid=(TILES // block,),
        in_specs=[
            whole(D, TILES), whole(D, TILES), part(TILES), part(D),
            pl.BlockSpec((1, block), lambda i: (0, i)), part(D), whole(16, D),
        ],
        out_specs=[part(D), whole(8, D)],
        out_shape=[shaped(TILES, D, BF), shaped(8, D, F32)],
        name="finish",
        compiler_params=params(40),
        cost_estimate=cost(TILES * TILES * D, 16 * MIB),
    )(back_a, back_b, order, start, mask_row, mid, vectors)


def exchange(value, axis, mask):
    pairs = [(source, source ^ mask) for source in range(lax.axis_size(axis))]
    return lax.ppermute(value, axis, pairs)


def after(value, *others):
    return lax.optimization_barrier((value,) + others)[0]


def after_all(values, *others):
    return lax.optimization_barrier(tuple(values) + others)[: len(values)]


def halve(value, dim, axis, bit):
    mine = lax.axis_index(axis) >> bit & 1
    half = value.shape[dim] // 2
    send = lax.dynamic_slice_in_dim(value, (1 - mine) * half, half, dim)
    keep = lax.dynamic_slice_in_dim(value, mine * half, half, dim)
    got = exchange(send, axis, 1 << bit)
    return (keep.astype(F32) + got.astype(F32)).astype(BF)


def join(value, dim, axis, bit):
    mine = lax.axis_index(axis) >> bit & 1
    got = exchange(value, axis, 1 << bit)
    first = jnp.where(mine == 0, value, got)
    second = jnp.where(mine == 0, got, value)
    return jnp.concatenate([first, second], axis=dim)


def log2_size(axis):
    return (lax.axis_size(axis) - 1).bit_length()


def reduce_blocks(blocks):
    value = blocks
    for bit in range(log2_size("dp")):
        value = halve(value, 1, "dp", bit)
    for bit in reversed(range(log2_size("seq"))):
        value = halve(value, 0, "seq", bit)
    value = value[0]
    for bit in reversed(range(log2_size("dp"))):
        value = join(value, 0, "dp", bit)
    return value.astype(F32)


def in_blocks(grad):
    count = lax.axis_size("seq")
    return grad.reshape(count, grad.shape[0] // count, -1)


def local(
    tokens, tile_mask, cotangent, qkv_weight, proj_weight, proj_bias, up_weight, up_bias,
    down_weight, down_bias, attn_gain, attn_shift, mlp_gain, mlp_shift, mask_vector,
):
    order = order_matrix()
    tables0 = weight_tables(0)
    query_table1 = weight_tables(1)[1]
    key_table1 = weight_tables(1, True)[0]
    tables2 = weight_tables(2)
    row = jnp.zeros((D,), BF)
    vectors = jnp.concatenate(
        [proj_bias, down_bias, attn_gain, attn_shift, mlp_gain, mlp_shift, mask_vector, row, up_bias,
         jnp.zeros((16 * D - 8 * D - up_bias.shape[0],), BF)]
    ).astype(F32).reshape(16, D)
    seq_count = lax.axis_size("seq")

    normed_t, start, token_squares, qkv, q4, q8, kv4, kvr = embed(
        tokens[0], tile_mask, vectors, qkv_weight, order
    )
    q2 = exchange(q4, "seq", 2)
    q3a = exchange(q8, "seq", 4)
    q3b = exchange(q8, "seq", 6)
    kv4_far = exchange(kv4, "seq", 1)
    kvr_far = exchange(after(kvr, kv4_far), "seq", 1)
    out0a, total0a = forward_own(qkv, tables0, 0)
    z2, z3a, z3b = forward_sent(q2, q3a, q3b, kv4, kv4_far, after_all(tables2, total0a))
    later = after_all(tables0, z2)
    z2 = exchange(z2, "seq", 2)
    z3a = exchange(z3a, "seq", 4)
    z3b = exchange(z3b, "seq", 6)
    out0b, total0b = forward_own(qkv, later, 1)
    out1, total1 = forward_pair(qkv, kv4_far, kvr_far, after(key_table1, total0b), query_table1)
    total0a, total0b = after_all((total0a, total0b), total1)
    attn_a, rest_a, total_a = merge(out0a, total0a, out1, total1, z2, z3a, z3b, 0)
    attn_b, rest_b, total_b = merge(out0b, total0b, out1, total1, z2, z3a, z3b, 1)

    layer_out, act, grad_pre, normed2, attn, grad_mid, feed_sums = feed(
        order, attn_a, attn_b, start, tile_mask, cotangent[0], vectors, proj_weight, up_weight, down_weight
    )
    grads_a, g4a, g8a = branch(grad_mid, proj_weight, order, attn_a, rest_a, total_a, 0)
    grads_b, g4b, g8b = branch(grad_mid, proj_weight, order, attn_b, rest_b, total_b, 1)
    g4, g8 = jnp.concatenate([g4a, g4b]), jnp.concatenate([g8a, g8b])
    grads = jnp.concatenate([grads_a, grads_b])
    g2 = exchange(g4, "seq", 2)
    g3a = exchange(g8, "seq", 4)
    g3b = exchange(g8, "seq", 6)
    early = weight_grads(act, cotangent[0], normed2, grad_pre, attn, after(grad_mid, g8))
    later = after(key_table1, early)
    early = lax.psum_scatter(early, ("seq", "dp"), scatter_dimension=0, tiled=True)
    dq1, dk1, dv1 = back_pair(qkv, grads, kv4_far, kvr_far, later, query_table1)
    dq2, dq3a, dq3b, dk4, dv4, far_a, far_b = back_sent(
        q2, q3a, q3b, g2, g3a, g3b, kv4, kv4_far, after_all(tables2, dq1), dk1, dv1
    )
    later = after_all(tables0, far_a)
    far_a = exchange(far_a, "seq", 1)
    far_b = exchange(far_b, "seq", 1)
    dq2 = exchange(dq2, "seq", 2)
    dq3a = exchange(dq3a, "seq", 4)
    dq3b = exchange(dq3b, "seq", 6)
    shared = (dq1, dq2, dq3a, dq3b, dk4, dv4)
    own_a = back_own(qkv, grads_a, later, 0)
    qkv_grad_a, back_a = collect(*own_a, *shared, far_a, normed_t, qkv_weight, 0)
    own_b = back_own(qkv, grads_b, after_all(tables0, qkv_grad_a), 1)
    qkv_grad_b, back_b = collect(*own_b, *shared, far_b, normed_t, qkv_weight, 1)
    early = after(early, qkv_grad_b)
    early = lax.all_gather(early, "dp", axis=0, tiled=True)
    tokens_grad, finish_sums = finish(back_a, back_b, order, start, tile_mask, grad_mid, vectors)

    share = D // seq_count
    ff = up_weight.shape[1]
    pieces = [finish_sums[:3].reshape(3, seq_count, share), feed_sums[4:8].reshape(4, seq_count, share)]
    small = jnp.transpose(jnp.concatenate(pieces), (1, 0, 2)).reshape(seq_count, 7 * share)
    everywhere = jnp.concatenate(
        [token_squares[0], feed_sums[8], feed_sums[9], 1.0 - tile_mask[0].astype(F32)]
    )
    small = jnp.concatenate(
        [small, feed_sums[: ff // D].reshape(seq_count, ff // seq_count),
         jnp.broadcast_to(everywhere[None], (seq_count, everywhere.shape[0]))],
        axis=1,
    )
    width = 3 * ROWS
    rows = 4 * -(-small.shape[1] // (4 * width))
    small = jnp.pad(small, ((0, 0), (0, rows * width - small.shape[1])))
    blocks = jnp.concatenate([in_blocks(qkv_grad_b), small.reshape(seq_count, rows, width).astype(BF)], axis=1)
    summed_a = reduce_blocks(in_blocks(qkv_grad_a))
    summed_b = reduce_blocks(blocks)
    qkv_grad = jnp.stack(
        [summed_a.reshape(share, 3, ROWS), summed_b[:share].reshape(share, 3, ROWS)], axis=2
    ).reshape(share, 3 * D)
    flat = summed_b[share:].reshape(-1)
    gain_grad, shift_grad, mask_grad, proj_bias_grad, down_bias_grad, gain2_grad, shift2_grad = (
        flat[i * share : (i + 1) * share] for i in range(7)
    )
    first = 7 * share
    up_bias_grad = flat[first : first + ff // seq_count]
    first = first + ff // seq_count
    squares = jnp.sum(flat[first : first + 3 * D].reshape(3, D), axis=1)
    count = jnp.sum(flat[first + 3 * D : first + 3 * D + TILES])
    stream_rms = jnp.sqrt(squares / (count * D))
    early = early.astype(F32)
    up_grad, proj_grad = early[:, :ff], early[:, ff : ff + D]
    down_grad = early[:, ff + D :].reshape(-1, D)
    return (
        layer_out[None], tokens_grad[None], qkv_grad, proj_grad, proj_bias_grad, up_grad, up_bias_grad,
        down_grad, down_bias_grad, gain_grad, shift_grad, gain2_grad, shift2_grad, mask_grad, stream_rms,
    )


def solution(mesh):
    rows = P("dp", "seq", None)
    in_specs = (rows, P("dp", "seq"), rows) + (P(),) * 12
    matrix, vector = P("seq", None), P("seq")
    out_specs = (
        rows, rows, matrix, matrix, vector, matrix, vector, matrix,
        vector, vector, vector, vector, vector, vector, P(),
    )
    return jax.shard_map(local, mesh=mesh, in_specs=in_specs, out_specs=out_specs, check_vma=False)
```

time: 3130 us -> 419 us (0.13)
  blocking collectives: 1100 us -> 0 us
  local copies, waits for them, and re-layouts: 1020 us -> 56.5 us
  matrix products: 547 us -> 0 us
  other arithmetic: 316 us -> 9.57 us
  Pallas kernels: 0 us -> 240 us
    unnamed x1 -> x0, blocking collectives: 1060 us -> none
    dot_general x222 -> x0, matrix products: 547 us -> none  [the longest x60 105 us: one_head(): jnp.dot(query_head, key_head.T, preferred_element_type=jnp.float32) * scale]
    broadcast_in_dim x39 -> x2, local copies, waits for them, and re-layouts: 310 us -> 0.01 us  [the longest x1 0.01 us: local(): jnp.broadcast_to(everywhere[None], (seq_count, everywhere.shape[0]))]
    pallas_call x0 -> x18, Pallas kernels: none -> 240 us  [the longest x2 45.1 us: back_own(): pl.pallas_call(back0_kernel, grid=(GROUP,), in_specs=[rows_of(HD, TILES,...]
    another operation x32 -> x2, local copies, waits for them, and re-layouts: 178 us -> 0.86 us  [local(): jnp.stack([summed_a.reshape(share, 3, ROWS), summed_b[:share].reshape(sha...]
    reshape x24 -> x10, local copies, waits for them, and re-layouts: 120 us -> 3.87 us  [the longest x1 1.62 us: local(): qkv_grad = jnp.stack([summed_a.reshape(share, 3, ROWS), summed_b[:share]....]
    convert_element_type x63 -> x10, other arithmetic: 95.7 us -> 3.13 us  [the longest x8 2.91 us: halve(): return (keep.astype(F32) + got.astype(F32)).astype(BF)]
    reduce_sum x72 -> x2, other arithmetic: 71.7 us -> 0.79 us  [the longest x1 0.67 us: local(): count = jnp.sum(flat[first + 3 * D:first + 3 * D + TILES])]
  transfers between devices with their start and end apart: 37 -> 32, of which waited for: 9 -> 12; matrix products, arithmetic and copies ran while one was open for 40% -> 4% of each run, Pallas kernels for 0% -> 36%
where the time goes in v1:
time: 419 us; the launch traced here: 415 us
  Pallas kernels  240 us (57%)
  waiting for transfers between devices  58 us (14%)
  local copies, waits for them, and re-layouts  56.5 us (13%)
  starting transfers between devices  35.6 us (8%)
  between operations  15.9 us (4%)
  other arithmetic  9.57 us (2%)
    ppermute x30, waiting for transfers between devices, exchange(): return lax.ppermute(value, axis, pairs)  47.5 us
    pallas_call x2, Pallas kernels, back_own(): pl.pallas_call(back0_kernel, grid=(GROUP,), in_specs=[rows_of(HD, TILES,...  45.1 us
    pallas_call x1, Pallas kernels, feed(): pl.pallas_call(feed_kernel, grid=(TILES // block,), in_specs=[part(TILES)...  44.3 us
    unnamed x158, local copies, waits for them, and re-layouts  41.3 us
    ppermute x30, starting transfers between devices, exchange(): return lax.ppermute(value, axis, pairs)  35.5 us
    pallas_call x2, Pallas kernels, forward_own(): pl.pallas_call(forward0_kernel, grid=(GROUP,), in_specs=[rows_of(HD, TILE...  30.9 us
    pallas_call x1, Pallas kernels, forward_pair(): pl.pallas_call(forward1_kernel, grid=(HEADS // 2,), in_specs=[pl.BlockSpe...  20.7 us
    pallas_call x1, Pallas kernels, weight_grads(): pl.pallas_call(weights_kernel, grid=(D // block,), in_specs=[pl.BlockSpec...  19.2 us
  transfers between devices with their start and end apart: 32, of which 12 were waited for; matrix products, arithmetic and copies ran while one was open for 4% of the time, Pallas kernels for 36%

profile of v1, /device:TPU:0, one launch (start us, length us, event | category | flops | bytes accessed | tf_op | source)
XLA Modules:
  0.0 415.4 jit_solution(9124612790600438517)
XLA Ops:
  14.9 12.9 %embed.1 = (bf16[768,1024]{1,0:T(8,128)(2,1)S(1)}, bf16[1024,768]{1,0:T(8,128)(2,1)S(1)}, f32[8,768]{1,0:T(8,128)S(1)}, bf16[2304,1024]{1,0:T(8,128)(2,1)}, bf16...) custom-call(bf16[1024,768]{1,0:T(8,128)(2,1)} %bitcast.22, ...), custom_call_target="tpu_custom_call" | custom-call | flops 5234491392 | bytes 20971520 | tf_op jit(solution)/shard_map/embed/pallas_call | solution.py:212
  28.7 1.1 copy-done.48
  29.8 5.1 %collective-permute-start.2 = (bf16[768,128]{1,0:T(8,128)(2,1)}, bf16[768,128]{1,0:T(8,128)(2,1)S(1)}, u32[]{:S(2)}, u32[]{:S(2)}) collective-permute-start(bf16[768,128]{1,0:T(8,128)(2,1)} %get-tuple-element.94), channel_id=1, source_target_pairs={{0,24},{4,28},{8,16},{12,20},{16,8},{20,12},{24,0},{28,4},{1,25},{... | collective-permute-start | bytes 589832 | tf_op jit(solution)/shard_map/ppermute | solution.py:904
  35.4 1.7 collective-permute-start.3
  37.1 2.3 copy-done.58
  39.5 15.4 %forward_own.2 = (f32[384,1024]{1,0:T(8,128)S(1)}, f32[8,1,1024]{2,1,0:T(1,128)S(1)}) custom-call(bf16[2304,1024]{1,0:T(8,128)(2,1)S(1)} %copy-done.58, bf16[2304,1024]{1,0:T(8,128)(2,1)S(1)} %copy-done.58, bf16[2304,1024]{1,0:T(8,128)(2,1)S(1)} %copy-done.58, bf16[128,1024]{1,0:T(8,128)(2,1)S(1)} %copy-done.40, bf16[128,1024]{1,0:T(8,128)(2,1)S(1)} %copy-done.37), custom_call_target="tpu_custom_call" | custom-call | flops 10066329600 | bytes 4194304 | tf_op jit(solution)/shard_map/forward_own/pallas_call | solution.py:354
  56.3 10.9 %forward_sent.1 = (bf16[1024,256]{1,0:T(8,128)(2,1)S(1)}, bf16[1024,128]{1,0:T(8,128)(2,1)S(1)}, bf16[1024,128]{1,0:T(8,128)(2,1)S(1)}) custom-call(bf16[768,256]{1,0:T(8,128)(2,1)} %collective-permute-done.q2_ref, bf16[768,128]{1,0:T(8,128)(2,1)} %collective-permute-done.1.q3a_ref, bf16[768,128]{1,0:T(8,128)(2,1)S(1)} %collective-permute-done.2.q3b_ref, ...), custom_call_target="tpu_custom_call" | custom-call | flops 3774873600 | bytes 4194304 | tf_op jit(solution)/shard_map/forward_sent/pallas_call | solution.py:404
  67.2 1.3 collective-permute-start.5
  69.0 2.9 collective-permute-start.6
  72.0 15.5 %forward_own.3 = (f32[384,1024]{1,0:T(8,128)S(1)}, f32[8,1,1024]{2,1,0:T(1,128)S(1)}) custom-call(bf16[2304,1024]{1,0:T(8,128)(2,1)S(1)} %bitcast.20, bf16[2304,1024]{1,0:T(8,128)(2,1)S(1)} %bitcast.20, bf16[2304,1024]{1,0:T(8,128)(2,1)S(1)} %bitcast.20, bf16[128,1024]{1,0:T(8,128)(2,1)S(1)} %copy-done.41, bf16[128,1024]{1,0:T(8,128)(2,1)S(1)} %copy-done.38), custom_call_target="tpu_custom_call" | custom-call | flops 10066329600 | bytes 4194304 | tf_op jit(solution)/shard_map/forward_own/pallas_call | solution.py:354
  87.5 20.7 %forward_pair.1 = (f32[768,512]{1,0:T(8,128)S(1)}, f32[16,1,512]{2,1,0:T(1,128)S(1)}) custom-call(bf16[2304,1024]{1,0:T(8,128)(2,1)S(1)} %bitcast.20, bf16[2304,1024]{1,0:T(8,128)(2,1)S(1)} %bitcast.20, bf16[1536,256]{1,0:T(8,128)(2,1)S(1)} %collective-permute-done.3.k4f_ref.v4f_ref.k8f_ref.v8f_ref.k4_ref.v4_ref, ...), custom_call_target="tpu_custom_call" | custom-call | flops 5033164800 | bytes 5242880 | tf_op jit(solution)/shard_map/forward_pair/pallas_call | solution.py:373
  111.0 44.3 %feed.1 = (bf16[1024,768]{1,0:T(8,128)(2,1)}, bf16[1024,3072]{1,0:T(8,128)(2,1)}, bf16[1024,3072]{1,0:T(8,128)(2,1)}, bf16[1024,768]{1,0:T(8,128)(2,1)}, bf16[10...) custom-call(bf16[1024,1024]{1,0:T(8,128)(2,1)} %constant.58.clone.order_ref, ...), custom_call_target="tpu_custom_call" | custom-call | flops 22145925120 | bytes 37748736 | tf_op jit(solution)/shard_map/feed/pallas_call | solution.py:522
  155.4 1.9 copy-done
  157.3 1.9 branch.2
  159.9 1.9 branch.3
  163.2 19.2 %weight_grads.1 = bf16[768,6912]{1,0:T(8,128)(2,1)} custom-call(bf16[1024,3072]{1,0:T(8,128)(2,1)} %get-tuple-element.127.act_ref, bf16[1024,768]{1,0:T(8,128)(2,1)S(1)} %bitcast.18, bf16[1024,768]{1,0:T(8,128)(2,1)S(1)} %copy-done.62, bf16[1024,3072]{1,0:T(8,128)(2,1)} %get-tuple-element.129.pre_ref, bf16[1024,768]{1,0:T(8,128)(2,1)S(1)} %copy-done.63, ...), custom_call_target="tpu_custom_call" | custom-call | flops 10871635968 | bytes 33554432 | tf_op jit(solution)/shard_map/weight_grads/pallas_call | solution.py:604
  182.5 3.9 collective-permute-start.10
  186.3 1.8 pad_maximum_fusion.2
  190.2 2.7 copy-done.59
  192.9 14.1 %back_pair.1 = (f32[768,512]{1,0:T(8,128)S(1)}, f32[768,512]{1,0:T(8,128)S(1)}, f32[768,512]{1,0:T(8,128)S(1)}) custom-call(bf16[2304,1024]{1,0:T(8,128)(2,1)S(1)} %copy-done.59, bf16[2304,1024]{1,0:T(8,128)(2,1)S(1)} %copy-done.59, bf16[1024,1024]{1,0:T(8,128)(2,1)S(1)} %pad_maximum_fusion.ga_ref.gb_ref, ...), custom_call_target="tpu_custom_call" | custom-call | flops 7549747200 | bytes 12582912 | tf_op jit(solution)/shard_map/back_pair/pallas_call | solution.py:722
  207.0 1.1 copy-done.51
  208.1 1.2 copy-done.64
  209.3 1.1 copy-done.66
  212.1 1.2 copy-done.25
  213.3 1.2 copy-done.28
  214.5 1.5 copy-done.65
  216.0 1.5 copy-done.67
  217.5 15.4 %back_sent.1 = (bf16[768,256]{1,0:T(8,128)(2,1)S(1)}, bf16[768,128]{1,0:T(8,128)(2,1)S(1)}, bf16[768,128]{1,0:T(8,128)(2,1)S(1)}, f32[768,256]{1,0:T(8,128)S(1)}...) custom-call(bf16[768,256]{1,0:T(8,128)(2,1)} %collective-permute-done.q2_ref, ...), custom_call_target="tpu_custom_call" | custom-call | flops 5662310400 | bytes 12582912 | tf_op jit(solution)/shard_map/back_sent/pallas_call | solution.py:740
  233.0 1.8 collective-permute-start.14
  234.8 2.0 collective-permute-start.12
  236.7 1.5 collective-permute-start.13
  239.3 2.6 copy-done.60
  242.0 22.5 %back_own.2 = (bf16[384,1024]{1,0:T(8,128)(2,1)S(1)}, bf16[384,1024]{1,0:T(8,128)(2,1)S(1)}, bf16[384,1024]{1,0:T(8,128)(2,1)S(1)}) custom-call(bf16[2304,1024]{1,0:T(8,128)(2,1)S(1)} %copy-done.60, bf16[512,1024]{1,0:T(8,128)(2,1)S(1)} %copy-done.12, bf16[2304,1024]{1,0:T(8,128)(2,1)S(1)} %copy-done.60, bf16[2304,1024]{1,0:T(8,128)(2,1)S(1)} %copy-done.60, ...), custom_call_target="tpu_custom_call" | custom-call | flops 15099494400 | bytes 7340032 | tf_op jit(solution)/shard_map/back_own/pallas_call | solution.py:767
  264.5 7.6 %collective-permute-done.11.dq2_ref = bf16[768,256]{1,0:T(8,128)(2,1)S(1)} collective-permute-done((bf16[768,256]{1,0:T(8,128)(2,1)S(1)}, bf16[768,256]{1,0:T(8,128)(2,1)S(1)}, u32[]{:S(2)}, u32[]{:S(2)}) %collective-permute-start.11) | collective-permute-done | bytes 393248 | tf_op jit(solution)/shard_map/ppermute | solution.py:904
  272.2 7.9 %collect.2 = (bf16[768,1152]{1,0:T(8,128)(2,1)S(1)}, f32[768,1024]{1,0:T(8,128)S(1)}) custom-call(bf16[384,1024]{1,0:T(8,128)(2,1)S(1)} %get-tuple-element.141.dq_ref, bf16[384,1024]{1,0:T(8,128)(2,1)S(1)} %get-tuple-element.142.dk_ref, bf16[384,1024]{1,0:T(8,128)(2,1)S(1)} %get-tuple-element.143.dv_ref, f32[768,512]{1,0:T(8,128)S(1)} %copy-done.52, ...), custom_call_target="tpu_custom_call" | custom-call | flops 3623878656 | bytes 16777216 | tf_op jit(solution)/shard_map/collect/pallas_call | solution.py:834
  280.1 1.1 constant_dynamic-slice_fusion.8
  281.2 2.6 copy-done.61
  283.8 22.5 %back_own.3 = (bf16[384,1024]{1,0:T(8,128)(2,1)S(1)}, bf16[384,1024]{1,0:T(8,128)(2,1)S(1)}, bf16[384,1024]{1,0:T(8,128)(2,1)S(1)}) custom-call(bf16[2304,1024]{1,0:T(8,128)(2,1)S(1)} %copy-done.61, bf16[512,1024]{1,0:T(8,128)(2,1)S(1)} %get-tuple-element.126.g_ref, bf16[2304,1024]{1,0:T(8,128)(2,1)S(1)} %copy-done.61, bf16[2304,1024]{1,0:T(8,128)(2,1)S(1)} %copy-done.61, ...), custom_call_target="tpu_custom_call" | custom-call | flops 15099494400 | bytes 7340032 | tf_op jit(solution)/shard_map/back_own/pallas_call | solution.py:767
  307.3 1.1 copy-done.34
  308.4 1.4 copy-done.50
  309.8 1.4 copy-done.53
  311.3 8.2 %collect.3 = (bf16[768,1152]{1,0:T(8,128)(2,1)S(1)}, f32[768,1024]{1,0:T(8,128)S(1)}) custom-call(bf16[384,1024]{1,0:T(8,128)(2,1)S(1)} %get-tuple-element.154.dq_ref, bf16[384,1024]{1,0:T(8,128)(2,1)S(1)} %get-tuple-element.155.dk_ref, bf16[384,1024]{1,0:T(8,128)(2,1)S(1)} %get-tuple-element.156.dv_ref, f32[768,512]{1,0:T(8,128)S(1)} %copy-done.53, ...), custom_call_target="tpu_custom_call" | custom-call | flops 3623878656 | bytes 16777216 | tf_op jit(solution)/shard_map/collect/pallas_call | solution.py:834
  319.5 1.2 copy-done.3
  320.7 5.5 %finish.1 = (bf16[1024,768]{1,0:T(8,128)(2,1)}, f32[8,768]{1,0:T(8,128)S(1)}) custom-call(f32[768,1024]{1,0:T(8,128)S(1)} %get-tuple-element.150.back_a_ref, f32[768,1024]{1,0:T(8,128)S(1)} %get-tuple-element.158.back_b_ref, bf16[1024,1024]{1,0:T(8,128)(2,1)S(1)} %copy-done.2, bf16[1024,768]{1,0:T(8,128)(2,1)S(1)} %copy-done.9, s32[1,1024]{1,0:T(1,128)S(1)} %copy-done.22, ...), custom_call_target="tpu_custom_call" | custom-call | flops 1610612736 | bytes 16777216 | tf_op jit(solution)/shard_map/finish/pallas_call | solution.py:887
  326.6 2.1 fusion
  330.2 1.5 add_convert_fusion.1
  331.8 1.7 collective-permute-start.17
  335.4 9.5 %collective-permute-done.17 = bf16[8,24,1152]{2,1,0:T(8,128)(2,1)S(1)} collective-permute-done((bf16[8,24,1152]{2,1,0:T(8,128)(2,1)S(1)}, bf16[8,24,1152]{2,1,0:T(8,128)(2,1)S(1)}, u32[]{:S(2)}, u32[]{:S(2)}) %collective-permute-start.17) | collective-permute-done | bytes 442400 | tf_op jit(solution)/shard_map/ppermute | solution.py:904
  345.0 1.1 collective-permute-start.18
  346.1 7.7 %collective-permute-done.24 = bf16[8,25,1152]{2,0,1:T(8,128)(2,1)S(1)} collective-permute-done((bf16[8,25,1152]{2,0,1:T(8,128)(2,1)S(1)}, bf16[8,25,1152]{2,0,1:T(8,128)(2,1)S(1)}, u32[]{:S(2)}, u32[]{:S(2)}) %collective-permute-start.24) | collective-permute-done | bytes 460832 | tf_op jit(solution)/shard_map/ppermute | solution.py:904
  355.1 1.2 collective-permute-done.18
  356.4 2.3 collective-permute-start.19
  358.7 10.8 %collective-permute-done.25 = bf16[4,25,1152]{2,1,0:T(8,128)(2,1)S(1)} collective-permute-done((bf16[4,25,1152]{2,1,0:T(8,128)(2,1)S(1)}, bf16[4,25,1152]{2,1,0:T(8,128)(2,1)S(1)}, u32[]{:S(2)}, u32[]{:S(2)}) %collective-permute-start.25) | collective-permute-done | bytes 230432 | tf_op jit(solution)/shard_map/ppermute | solution.py:904
  370.2 3.6 collective-permute-done.20
  373.9 1.6 collective-permute-start.21
  375.8 1.3 collective-permute-start.27
  378.1 2.1 collective-permute-done.27
  380.2 1.6 collective-permute-start.28
  381.9 2.7 collective-permute-done.28
  388.2 1.6 reshape.109
  392.4 10.5 %all-gather.2.cloned.1.call-done = bf16[96,6912]{1,0:T(8,128)(2,1)} async-done(((bf16[24,6912]{1,0:T(8,128)(2,1)}), bf16[96,6912]{1,0:T(8,128)(2,1)}) %all-gather.2.cloned.1.call-update) | async-done | bytes 1327120 | tf_op jit(solution)/shard_map/all_gather | solution.py:1018
  402.9 2.5 fusion.4
  405.4 1.3 reshape.111
  406.8 1.6 slice.91
  (253 shorter events, 34.5 us)
Async XLA Ops:
  7.2 377.6 %reduce-scatter.2.cloned.1.call-start = ((), (), s32[]{:S(2)}) async-start(), calls=%async_computation.1 | async-start | bytes 10948608 | tf_op jit(solution)/shard_map/reduce_scatter | solution.py:1001
  14.9 22.2 %copy-start.37 = (bf16[128,1024]{1,0:T(8,128)(2,1)S(1)}, bf16[128,1024]{1,0:T(8,128)(2,1)}, u32[]{:S(2)}) copy-start(bf16[128,1024]{1,0:T(8,128)(2,1)} %constant.60.clone.qt_ref) | copy-start | bytes 786436
  14.9 22.2 %copy-start.40 = (bf16[128,1024]{1,0:T(8,128)(2,1)S(1)}, bf16[128,1024]{1,0:T(8,128)(2,1)}, u32[]{:S(2)}) copy-start(bf16[128,1024]{1,0:T(8,128)(2,1)} %constant.59.clone.kt_ref) | copy-start | bytes 786436
  29.8 25.1 %copy-start.8 = (bf16[1024,768]{1,0:T(8,128)(2,1)}, bf16[1024,768]{1,0:T(8,128)(2,1)S(1)}, u32[]{:S(2)}) copy-start(bf16[1024,768]{1,0:T(8,128)(2,1)S(1)} %get-tuple-element.114.start_ref) | copy-start | bytes 4718596
  29.8 26.4 %copy-start.24 = (bf16[1536,256]{1,0:T(8,128)(2,1)}, bf16[1536,256]{1,0:T(8,128)(2,1)S(1)}, u32[]{:S(2)}) copy-start(bf16[1536,256]{1,0:T(8,128)(2,1)S(1)} %get-tuple-element.95.k4_ref.v4_ref.k8_ref.v8_ref) | copy-start | bytes 2359300
  29.8 26.4 %collective-permute-start.2 = (bf16[768,128]{1,0:T(8,128)(2,1)}, bf16[768,128]{1,0:T(8,128)(2,1)S(1)}, u32[]{:S(2)}, u32[]{:S(2)}) collective-permute-start(bf16[768,128]{1,0:T(8,128)(2,1)} %get-tuple-element.94), channel_id=1, source_target_pairs={{0,24},{4,28},{8,16},{12,20},{16,8},{20,12},{24,0},{28,4},{1,25},{... | collective-permute-start | bytes 589832 | tf_op jit(solution)/shard_map/ppermute | solution.py:904
  34.9 21.3 %collective-permute-start.1 = (bf16[768,128]{1,0:T(8,128)(2,1)}, bf16[768,128]{1,0:T(8,128)(2,1)}, u32[]{:S(2)}, u32[]{:S(2)}) collective-permute-start(bf16[768,128]{1,0:T(8,128)(2,1)} %get-tuple-element.94), channel_id=1, source_target_pairs={{0,16},{4,20},{8,24},{12,28},{16,0},{20,4},{24,8},{28,12},{1,17},{... | collective-permute-start | bytes 589832 | tf_op jit(solution)/shard_map/ppermute | solution.py:904
  34.9 21.3 %collective-permute-start = (bf16[768,256]{1,0:T(8,128)(2,1)}, bf16[768,256]{1,0:T(8,128)(2,1)}, u32[]{:S(2)}, u32[]{:S(2)}) collective-permute-start(bf16[768,256]{1,0:T(8,128)(2,1)} %get-tuple-element.93), channel_id=1, source_target_pairs={{0,8},{4,12},{8,0},{12,4},{16,24},{20,28},{24,16},{28,20},{1,9},{5... | collective-permute-start | bytes 1179656 | tf_op jit(solution)/shard_map/ppermute | solution.py:904
  35.4 20.8 %collective-permute-start.3 = (bf16[1536,256]{1,0:T(8,128)(2,1)S(1)}, bf16[1536,256]{1,0:T(8,128)(2,1)S(1)}, u32[]{:S(2)}, u32[]{:S(2)}) collective-permute-start(bf16[1536,256]{1,0:T(8,128)(2,1)S(1)} %get-tuple-element.95.k4_ref.v4_ref.k8_ref.v8_ref), channel_id=1, source_target_pairs={{0,4},{4,0},{8,12},{12,8},{16,20},{20,16},{24,28},{28,24},{1,5},{5... | collective-permute-start | bytes 2359304 | tf_op jit(solution)/shard_map/ppermute | solution.py:904
  39.5 16.1 %copy-start.21 = (s32[1,1024]{1,0:T(1,128)S(1)}, s32[1,1024]{1,0:T(1,128)}, u32[]{:S(2)}) copy-start(s32[1,1024]{1,0:T(1,128)} %mask_ref.5) | copy-start | bytes 12292
  39.5 16.7 %copy-start.46 = (bf16[32,256]{1,0:T(8,128)(2,1)S(1)}, bf16[32,256]{1,0:T(8,128)(2,1)}, u32[]{:S(2)}) copy-start(bf16[32,256]{1,0:T(8,128)(2,1)} %constant.64.clone.qt_ref) | copy-start | bytes 49156
  39.5 16.8 %copy-start.47 = (bf16[32,256]{1,0:T(8,128)(2,1)S(1)}, bf16[32,256]{1,0:T(8,128)(2,1)}, u32[]{:S(2)}) copy-start(bf16[32,256]{1,0:T(8,128)(2,1)} %constant.63.clone.kt_ref) | copy-start | bytes 49156
  55.6 16.4 %slice-start = ((s8[4718592]{0:T(1024)(128)(4,1)}), s8[4194304]{0:T(1024)(128)(4,1)S(1)}, s32[]{:S(2)}) async-start(s8[4718592]{0:T(1024)(128)(4,1)} %bitcast.19), calls=%async_computation.3 | async-start | bytes 8388608
  56.2 15.8 %copy-start.38 = (bf16[128,1024]{1,0:T(8,128)(2,1)S(1)}, bf16[128,1024]{1,0:T(8,128)(2,1)}, u32[]{:S(2)}) copy-start(bf16[128,1024]{1,0:T(8,128)(2,1)} %constant.60.clone.qt_ref) | copy-start | bytes 786436
  56.2 15.8 %copy-start.41 = (bf16[128,1024]{1,0:T(8,128)(2,1)S(1)}, bf16[128,1024]{1,0:T(8,128)(2,1)}, u32[]{:S(2)}) copy-start(bf16[128,1024]{1,0:T(8,128)(2,1)} %constant.59.clone.kt_ref) | copy-start | bytes 786436
  56.2 15.8 %slice-start.1 = ((s8[4718592]{0:T(1024)(128)(4,1)}), s8[524288]{0:T(1024)(128)(4,1)S(1)}, s32[]{:S(2)}) async-start(s8[4718592]{0:T(1024)(128)(4,1)} %bitcast.19), calls=%async_computation.4 | async-start | bytes 1048576
  56.2 31.2 %copy-start.26 = (bf16[1536,256]{1,0:T(8,128)(2,1)}, bf16[1536,256]{1,0:T(8,128)(2,1)S(1)}, u32[]{:S(2)}) copy-start(bf16[1536,256]{1,0:T(8,128)(2,1)S(1)} %collective-permute-done.3.k4f_ref.v4f_ref.k8f_ref.v8f_ref.k4_ref.v4_ref) | copy-start | bytes 2359300
  67.2 41.1 %collective-permute-start.5 = (bf16[1024,256]{1,0:T(8,128)(2,1)S(1)}, bf16[1024,256]{1,0:T(8,128)(2,1)S(1)}, u32[]{:S(2)}, u32[]{:S(2)}) collective-permute-start(bf16[1024,256]{1,0:T(8,128)(2,1)S(1)} %get-tuple-element.98), channel_id=1, source_target_pairs={{0,8},{4,12},{8,0},{12,4},{16,24},{20,28},{24,16},{28,20},{1,9},{5... | collective-permute-start | bytes 1572872 | tf_op jit(solution)/shard_map/ppermute | solution.py:904
  68.5 19.0 %collective-permute-start.4 = (bf16[1536,256]{1,0:T(8,128)(2,1)S(1)}, bf16[1536,256]{1,0:T(8,128)(2,1)S(1)}, u32[]{:S(2)}, u32[]{:S(2)}) collective-permute-start(bf16[1536,256]{1,0:T(8,128)(2,1)S(1)} %copy-done.32), channel_id=1, source_target_pairs={{0,4},{4,0},{8,12},{12,8},{16,20},{20,16},{24,28},{28,24},{1,5},{5... | collective-permute-start | bytes 2359304 | tf_op jit(solution)/shard_map/ppermute | solution.py:904
  69.0 39.2 %collective-permute-start.6 = (bf16[1024,128]{1,0:T(8,128)(2,1)S(1)}, bf16[1024,128]{1,0:T(8,128)(2,1)S(1)}, u32[]{:S(2)}, u32[]{:S(2)}) collective-permute-start(bf16[1024,128]{1,0:T(8,128)(2,1)S(1)} %get-tuple-element.108), channel_id=1, source_target_pairs={{0,16},{4,20},{8,24},{12,28},{16,0},{20,4},{24,8},{28,12},{1,17},{... | collective-permute-start | bytes 786440 | tf_op jit(solution)/shard_map/ppermute | solution.py:904
  72.0 15.5 %copy-start.43 = (bf16[64,512]{1,0:T(8,128)(2,1)S(1)}, bf16[64,512]{1,0:T(8,128)(2,1)}, u32[]{:S(2)}) copy-start(bf16[64,512]{1,0:T(8,128)(2,1)} %constant.62.clone.kt_ref) | copy-start | bytes 196612
  72.0 15.5 %copy-start.44 = (bf16[64,512]{1,0:T(8,128)(2,1)S(1)}, bf16[64,512]{1,0:T(8,128)(2,1)}, u32[]{:S(2)}) copy-start(bf16[64,512]{1,0:T(8,128)(2,1)} %constant.61.clone.qt_ref) | copy-start | bytes 196612
  72.0 36.3 %collective-permute-start.7 = (bf16[1024,128]{1,0:T(8,128)(2,1)S(1)}, bf16[1024,128]{1,0:T(8,128)(2,1)S(1)}, u32[]{:S(2)}, u32[]{:S(2)}) collective-permute-start(bf16[1024,128]{1,0:T(8,128)(2,1)S(1)} %get-tuple-element.109), channel_id=1, source_target_pairs={{0,24},{4,28},{8,16},{12,20},{16,8},{20,12},{24,0},{28,4},{1,25},{... | collective-permute-start | bytes 786440 | tf_op jit(solution)/shard_map/ppermute | solution.py:904
  87.5 20.7 %copy-start.29 = (bf16[1536,256]{1,0:T(8,128)(2,1)}, bf16[1536,256]{1,0:T(8,128)(2,1)S(1)}, u32[]{:S(2)}) copy-start(bf16[1536,256]{1,0:T(8,128)(2,1)S(1)} %collective-permute-done.4.kr_ref.vr_ref) | copy-start | bytes 2359300
  111.0 44.3 %copy-start.2 = (bf16[1024,1024]{1,0:T(8,128)(2,1)S(1)}, bf16[1024,1024]{1,0:T(8,128)(2,1)}, u32[]{:S(2)}) copy-start(bf16[1024,1024]{1,0:T(8,128)(2,1)} %constant.58.clone.order_ref) | copy-start | bytes 6291460
  111.0 44.4 %copy-start.5 = (bf16[768,768]{1,0:T(8,128)(2,1)S(1)}, bf16[768,768]{1,0:T(8,128)(2,1)}, u32[]{:S(2)}) copy-start(bf16[768,768]{1,0:T(8,128)(2,1)} %proj_ref.5) | copy-start | bytes 3538948
  111.0 44.4 %copy-start.16 = (bf16[384,1024]{1,0:T(8,128)(2,1)S(1)}, bf16[384,1024]{1,0:T(8,128)(2,1)}, u32[]{:S(2)}) copy-start(bf16[384,1024]{1,0:T(8,128)(2,1)} %copy-done.15) | copy-start | bytes 2359300
  182.4 220.5 %all-gather.2.cloned.1.call-start = ((), (), s32[]{:S(2)}) async-start(), calls=%async_computation.2 | async-start | bytes 1658880 | tf_op jit(solution)/shard_map/all_gather | solution.py:1018
  182.5 29.6 %collective-permute-start.10 = (bf16[1024,128]{1,0:T(8,128)(2,1)}, bf16[1024,128]{1,0:T(8,128)(2,1)}, u32[]{:S(2)}, u32[]{:S(2)}) collective-permute-start(bf16[1024,128]{1,0:T(8,128)(2,1)} %constant_dynamic-update-slice_fusion.2), channel_id=1, source_target_pairs={{0,24},{4,28},{8,16},{12,20},{16,8},{20,12},{24,0},{28,4},{1,25},{... | collective-permute-start | bytes 786440 | tf_op jit(solution)/shard_map/ppermute | solution.py:904
  186.3 25.7 %collective-permute-start.9 = (bf16[1024,128]{1,0:T(8,128)(2,1)}, bf16[1024,128]{1,0:T(8,128)(2,1)}, u32[]{:S(2)}, u32[]{:S(2)}) collective-permute-start(bf16[1024,128]{1,0:T(8,128)(2,1)} %constant_dynamic-update-slice_fusion.2), channel_id=1, source_target_pairs={{0,16},{4,20},{8,24},{12,28},{16,0},{20,4},{24,8},{28,12},{1,17},{... | collective-permute-start | bytes 786440 | tf_op jit(solution)/shard_map/ppermute | solution.py:904
  188.1 24.0 %collective-permute-start.8 = (bf16[1024,256]{1,0:T(8,128)(2,1)}, bf16[1024,256]{1,0:T(8,128)(2,1)}, u32[]{:S(2)}, u32[]{:S(2)}) collective-permute-start(bf16[1024,256]{1,0:T(8,128)(2,1)} %pad_maximum_fusion.2), channel_id=1, source_target_pairs={{0,8},{4,12},{8,0},{12,4},{16,24},{20,28},{24,16},{28,20},{1,9},{5... | collective-permute-start | bytes 1572872 | tf_op jit(solution)/shard_map/ppermute | solution.py:904
  192.9 17.6 %copy-start.68 = (f32[16,768]{1,0:T(8,128)S(1)}, f32[16,768]{1,0:T(8,128)}, u32[]{:S(2)}) copy-start(f32[16,768]{1,0:T(8,128)} %get-tuple-element.162) | copy-start | bytes 147460
  192.9 19.1 %copy-start.70 = (f32[1,1024]{1,0:T(1,128)S(1)}, f32[1,1024]{1,0:T(1,128)}, u32[]{:S(2)}) copy-start(f32[1,1024]{1,0:T(1,128)} %convert_subtract_fusion) | copy-start | bytes 12292
  192.9 19.2 %copy-start.71 = (bf16[768]{0:T(1024)(128)(2,1)S(1)}, bf16[768]{0:T(1024)(128)(2,1)}, u32[]{:S(2)}) copy-start(bf16[768]{0:T(1024)(128)(2,1)} %slice_reduce_fusion.3) | copy-start | bytes 4612
  192.9 19.2 %copy-start.36 = (bf16[768,128]{1,0:T(8,128)(2,1)S(1)}, bf16[768,128]{1,0:T(8,128)(2,1)}, u32[]{:S(2)}) copy-start(bf16[768,128]{1,0:T(8,128)(2,1)} %copy-done.35) | copy-start | bytes 589828
  217.5 21.8 %copy-start.12 = (bf16[512,1024]{1,0:T(8,128)(2,1)S(1)}, bf16[512,1024]{1,0:T(8,128)(2,1)}, u32[]{:S(2)}) copy-start(bf16[512,1024]{1,0:T(8,128)(2,1)} %copy-done.10) | copy-start | bytes 3145732
  217.5 21.8 %copy-start.39 = (bf16[128,1024]{1,0:T(8,128)(2,1)S(1)}, bf16[128,1024]{1,0:T(8,128)(2,1)}, u32[]{:S(2)}) copy-start(bf16[128,1024]{1,0:T(8,128)(2,1)} %constant.60.clone.qt_ref) | copy-start | bytes 786436
  217.5 21.8 %copy-start.42 = (bf16[128,1024]{1,0:T(8,128)(2,1)S(1)}, bf16[128,1024]{1,0:T(8,128)(2,1)}, u32[]{:S(2)}) copy-start(bf16[128,1024]{1,0:T(8,128)(2,1)} %constant.59.clone.kt_ref) | copy-start | bytes 786436
  232.9 39.2 %copy-start.54 = (f32[768,256]{1,0:T(8,128)}, f32[768,256]{1,0:T(8,128)S(1)}, u32[]{:S(2)}) copy-start(f32[768,256]{1,0:T(8,128)S(1)} %get-tuple-element.147.dk4_ref) | copy-start | bytes 2359300
  233.0 39.2 %copy-start.56 = (f32[768,256]{1,0:T(8,128)}, f32[768,256]{1,0:T(8,128)S(1)}, u32[]{:S(2)}) copy-start(f32[768,256]{1,0:T(8,128)S(1)} %get-tuple-element.148.dv4_ref) | copy-start | bytes 2359300
  233.0 39.2 %collective-permute-start.14 = (bf16[2,384,512]{2,1,0:T(8,128)(2,1)S(1)}, bf16[2,384,512]{2,1,0:T(8,128)(2,1)S(1)}, u32[]{:S(2)}, u32[]{:S(2)}) collective-permute-start(bf16[2,384,512]{2,1,0:T(8,128)(2,1)S(1)} %get-tuple-element.138), channel_id=1, source_target_pairs={{0,4},{4,0},{8,12},{12,8},{16,20},{20,16},{24,28},{28,24},{1,5},{5... | collective-permute-start | bytes 2359304 | tf_op jit(solution)/shard_map/ppermute | solution.py:904
  234.8 29.8 %collective-permute-start.12 = (bf16[768,128]{1,0:T(8,128)(2,1)S(1)}, bf16[768,128]{1,0:T(8,128)(2,1)S(1)}, u32[]{:S(2)}, u32[]{:S(2)}) collective-permute-start(bf16[768,128]{1,0:T(8,128)(2,1)S(1)} %get-tuple-element.145), channel_id=1, source_target_pairs={{0,16},{4,20},{8,24},{12,28},{16,0},{20,4},{24,8},{28,12},{1,17},{... | collective-permute-start | bytes 589832 | tf_op jit(solution)/shard_map/ppermute | solution.py:904
  236.7 27.8 %collective-permute-start.13 = (bf16[768,128]{1,0:T(8,128)(2,1)S(1)}, bf16[768,128]{1,0:T(8,128)(2,1)S(1)}, u32[]{:S(2)}, u32[]{:S(2)}) collective-permute-start(bf16[768,128]{1,0:T(8,128)(2,1)S(1)} %get-tuple-element.146), channel_id=1, source_target_pairs={{0,24},{4,28},{8,16},{12,20},{16,8},{20,12},{24,0},{28,4},{1,25},{... | collective-permute-start | bytes 589832 | tf_op jit(solution)/shard_map/ppermute | solution.py:904
  238.2 33.9 %collective-permute-start.11 = (bf16[768,256]{1,0:T(8,128)(2,1)S(1)}, bf16[768,256]{1,0:T(8,128)(2,1)S(1)}, u32[]{:S(2)}, u32[]{:S(2)}) collective-permute-start(bf16[768,256]{1,0:T(8,128)(2,1)S(1)} %get-tuple-element.144), channel_id=1, source_target_pairs={{0,8},{4,12},{8,0},{12,4},{16,24},{20,28},{24,16},{28,20},{1,9},{5... | collective-permute-start | bytes 1179656 | tf_op jit(solution)/shard_map/ppermute | solution.py:904
  238.7 33.4 %copy-start.49 = (bf16[768,1024]{1,0:T(8,128)(2,1)S(1)}, bf16[768,1024]{1,0:T(8,128)(2,1)}, u32[]{:S(2)}) copy-start(bf16[768,1024]{1,0:T(8,128)(2,1)} %copy-done.48) | copy-start | bytes 4718596
  238.7 33.4 %copy-start.52 = (f32[768,512]{1,0:T(8,128)S(1)}, f32[768,512]{1,0:T(8,128)}, u32[]{:S(2)}) copy-start(f32[768,512]{1,0:T(8,128)} %copy-done.51) | copy-start | bytes 4718596
  238.8 67.6 %collective-permute-start.15 = (bf16[2,384,512]{2,1,0:T(8,128)(2,1)S(1)}, bf16[2,384,512]{2,1,0:T(8,128)(2,1)S(1)}, u32[]{:S(2)}, u32[]{:S(2)}) collective-permute-start(bf16[2,384,512]{2,1,0:T(8,128)(2,1)S(1)} %get-tuple-element.157), channel_id=1, source_target_pairs={{0,4},{4,0},{8,12},{12,8},{16,20},{20,16},{24,28},{28,24},{1,5},{5... | collective-permute-start | bytes 2359304 | tf_op jit(solution)/shard_map/ppermute | solution.py:904
  280.0 26.3 %copy-start.6 = (bf16[768,1152]{1,0:T(8,128)(2,1)}, bf16[768,1152]{1,0:T(8,128)(2,1)S(1)}, u32[]{:S(2)}) copy-start(bf16[768,1152]{1,0:T(8,128)(2,1)S(1)} %get-tuple-element.151) | copy-start | bytes 5308420
  281.1 26.1 %copy-start.55 = (f32[768,256]{1,0:T(8,128)S(1)}, f32[768,256]{1,0:T(8,128)}, u32[]{:S(2)}) copy-start(f32[768,256]{1,0:T(8,128)} %copy-done.54) | copy-start | bytes 2359300
  281.2 26.1 %copy-start.57 = (f32[768,256]{1,0:T(8,128)S(1)}, f32[768,256]{1,0:T(8,128)}, u32[]{:S(2)}) copy-start(f32[768,256]{1,0:T(8,128)} %copy-done.56) | copy-start | bytes 2359300
  281.2 49.0 %collective-permute-start.16 = (bf16[8,48,1152]{2,1,0:T(8,128)(2,1)}, bf16[8,48,1152]{2,1,0:T(8,128)(2,1)}, u32[]{:S(2)}, u32[]{:S(2)}) collective-permute-start(bf16[8,48,1152]{2,1,0:T(8,128)(2,1)} %constant_dynamic-slice_fusion.8), channel_id=1, source_target_pairs={{0,1},{1,0},{2,3},{3,2},{4,5},{5,4},{6,7},{7,6},{8,9},{9,8},{10,11... | collective-permute-start | bytes 2654216 | tf_op jit(solution)/shard_map/ppermute | solution.py:904
  329.7 3.7 collective-permute-start.23
  331.8 13.1 %collective-permute-start.17 = (bf16[8,24,1152]{2,1,0:T(8,128)(2,1)S(1)}, bf16[8,24,1152]{2,1,0:T(8,128)(2,1)S(1)}, u32[]{:S(2)}, u32[]{:S(2)}) collective-permute-start(bf16[8,24,1152]{2,1,0:T(8,128)(2,1)S(1)} %constant_dynamic-slice_fusion.7), channel_id=1, source_target_pairs={{0,2},{1,3},{2,0},{3,1},{4,6},{5,7},{6,4},{7,5},{8,10},{9,11},{10,... | collective-permute-start | bytes 1327112 | tf_op jit(solution)/shard_map/ppermute | solution.py:904
  334.6 19.2 %collective-permute-start.24 = (bf16[8,25,1152]{2,0,1:T(8,128)(2,1)S(1)}, bf16[8,25,1152]{2,0,1:T(8,128)(2,1)S(1)}, u32[]{:S(2)}, u32[]{:S(2)}) collective-permute-start(bf16[8,25,1152]{2,0,1:T(8,128)(2,1)S(1)} %copy.60), channel_id=1, source_target_pairs={{0,2},{1,3},{2,0},{3,1},{4,6},{5,7},{6,4},{7,5},{8,10},{9,11},{10,... | collective-permute-start | bytes 1382408 | tf_op jit(solution)/shard_map/ppermute | solution.py:904
  345.0 11.3 %collective-permute-start.18 = (bf16[4,24,1152]{2,1,0:T(8,128)(2,1)S(1)}, bf16[4,24,1152]{2,1,0:T(8,128)(2,1)S(1)}, u32[]{:S(2)}, u32[]{:S(2)}) collective-permute-start(bf16[4,24,1152]{2,1,0:T(8,128)(2,1)S(1)} %constant_dynamic-slice_fusion.6), channel_id=1, source_target_pairs={{0,16},{4,20},{8,24},{12,28},{16,0},{20,4},{24,8},{28,12},{1,17},{... | collective-permute-start | bytes 663560 | tf_op jit(solution)/shard_map/ppermute | solution.py:904
  354.1 15.4 %collective-permute-start.25 = (bf16[4,25,1152]{2,1,0:T(8,128)(2,1)S(1)}, bf16[4,25,1152]{2,1,0:T(8,128)(2,1)S(1)}, u32[]{:S(2)}, u32[]{:S(2)}) collective-permute-start(bf16[4,25,1152]{2,1,0:T(8,128)(2,1)S(1)} %constant_dynamic-slice_fusion.2), channel_id=1, source_target_pairs={{0,16},{4,20},{8,24},{12,28},{16,0},{20,4},{24,8},{28,12},{1,17},{... | collective-permute-start | bytes 691208 | tf_op jit(solution)/shard_map/ppermute | solution.py:904
  356.4 13.1 %collective-permute-start.19 = (bf16[2,24,1152]{2,1,0:T(8,128)(2,1)S(1)}, bf16[2,24,1152]{2,1,0:T(8,128)(2,1)S(1)}, u32[]{:S(2)}, u32[]{:S(2)}) collective-permute-start(bf16[2,24,1152]{2,1,0:T(8,128)(2,1)S(1)} %constant_dynamic-slice_fusion.5), channel_id=1, source_target_pairs={{0,8},{4,12},{8,0},{12,4},{16,24},{20,28},{24,16},{28,20},{1,9},{5... | collective-permute-start | bytes 331784 | tf_op jit(solution)/shard_map/ppermute | solution.py:904
  369.6 4.2 %collective-permute-start.20 = (bf16[1,24,1152]{2,1,0:T(8,128)(2,1)S(1)}, bf16[1,24,1152]{2,1,0:T(8,128)(2,1)S(1)}, u32[]{:S(2)}, u32[]{:S(2)}) collective-permute-start(bf16[1,24,1152]{2,1,0:T(8,128)(2,1)S(1)} %constant_dynamic-slice_fusion.4), channel_id=1, source_target_pairs={{0,4},{4,0},{8,12},{12,8},{16,20},{20,16},{24,28},{28,24},{1,5},{5... | collective-permute-start | bytes 165896 | tf_op jit(solution)/shard_map/ppermute | solution.py:904
  370.2 5.6 %collective-permute-start.26 = (bf16[2,25,1152]{2,1,0:T(8,128)(2,1)S(1)}, bf16[2,25,1152]{2,1,0:T(8,128)(2,1)S(1)}, u32[]{:S(2)}, u32[]{:S(2)}) collective-permute-start(bf16[2,25,1152]{2,1,0:T(8,128)(2,1)S(1)} %constant_dynamic-slice_fusion.1), channel_id=1, source_target_pairs={{0,8},{4,12},{8,0},{12,4},{16,24},{20,28},{24,16},{28,20},{1,9},{5... | collective-permute-start | bytes 345608 | tf_op jit(solution)/shard_map/ppermute | solution.py:904
  373.9 4.2 %collective-permute-start.21 = (bf16[24,1152]{1,0:T(8,128)(2,1)S(1)}, bf16[24,1152]{1,0:T(8,128)(2,1)S(1)}, u32[]{:S(2)}, u32[]{:S(2)}) collective-permute-start(bf16[24,1152]{1,0:T(8,128)(2,1)S(1)} %fusion.3), channel_id=1, source_target_pairs={{0,2},{1,3},{2,0},{3,1},{4,6},{5,7},{6,4},{7,5},{8,10},{9,11},{10,... | collective-permute-start | bytes 165896 | tf_op jit(solution)/shard_map/ppermute | solution.py:904
  375.8 4.4 %collective-permute-start.27 = (bf16[1,25,1152]{2,1,0:T(8,128)(2,1)S(1)}, bf16[1,25,1152]{2,1,0:T(8,128)(2,1)S(1)}, u32[]{:S(2)}, u32[]{:S(2)}) collective-permute-start(bf16[1,25,1152]{2,1,0:T(8,128)(2,1)S(1)} %constant_dynamic-slice_fusion), channel_id=1, source_target_pairs={{0,4},{4,0},{8,12},{12,8},{16,20},{20,16},{24,28},{28,24},{1,5},{5... | collective-permute-start | bytes 172808 | tf_op jit(solution)/shard_map/ppermute | solution.py:904
  380.2 4.4 %collective-permute-start.28 = (bf16[25,1152]{1,0:T(8,128)(2,1)S(1)}, bf16[25,1152]{1,0:T(8,128)(2,1)S(1)}, u32[]{:S(2)}, u32[]{:S(2)}) collective-permute-start(bf16[25,1152]{1,0:T(8,128)(2,1)S(1)} %fusion.2), channel_id=1, source_target_pairs={{0,2},{1,3},{2,0},{3,1},{4,6},{5,7},{6,4},{7,5},{8,10},{9,11},{10,... | collective-permute-start | bytes 172808 | tf_op jit(solution)/shard_map/ppermute | solution.py:904
  381.9 3.0 collective-permute-start.22
  384.7 1.4 collective-permute-start.29
  (42 other events, 145.0 us)
Sparse Core Ops, SparseCore 0:
  182.5 157.8 reduce-scatter.1
  385.0 17.9 all-gather.1
